TPU v7x, 32 devices: a whole 2x2x4 slice. The times are simulated.
32 devices in a mesh: grp: 4 (over y, x), tok: 8 (over z, core).
Axes of the slice: x: 2, y: 2, z: 4, core: 2. Of those that a mesh axis runs over, the one named last changes fastest.
Arguments:
- tokens: bfloat16 [4096, 2560], P(('grp', 'tok')), may hold values from -6 to 6
- input_gain: bfloat16 [2560], replicated, may hold values from 0.25 to 1.75
- query_down: bfloat16 [2560, 768], replicated, may hold values from -0.125 to 0.125
- query_gain: bfloat16 [768], replicated, may hold values from 0.25 to 1.75
- query_up: bfloat16 [768, 1920], replicated, may hold values from -0.21875 to 0.21875
- latent_down: bfloat16 [2560, 288], replicated, may hold values from -0.125 to 0.125
- latent_gain: bfloat16 [256], replicated, may hold values from 0.25 to 1.75
- key_up: bfloat16 [256, 1280], replicated, may hold values from -0.375 to 0.375
- value_up: bfloat16 [256, 1280], replicated, may hold values from -0.375 to 0.375
- output_weight: bfloat16 [1280, 2560], replicated, may hold values from -0.15625 to 0.15625
- post_gain: bfloat16 [2560], replicated, may hold values from 0.25 to 1.75
- gate_weight: bfloat16 [2560, 3200], P('tok', 'grp'), may hold values from -0.125 to 0.125
- up_weight: bfloat16 [2560, 3200], P('tok', 'grp'), may hold values from -0.125 to 0.125
- down_weight: bfloat16 [3200, 2560], P('grp', 'tok'), may hold values from -0.109375 to 0.109375
- cache_latents: bfloat16 [4, 4096, 288], P('grp', 'tok'), as said below
- prompt_latents: bfloat16 [8, 1024, 288], P(None, 'tok'), as said below
- cache_len: int32 [4], replicated, may hold values from 1 to 4096, 8192 in all
- prompt_len: int32 [8], replicated, may hold values from 1 to 1024, 4096 in all
- prompt_of: int32 [4], replicated, may hold values from 0 to 7
Outputs:
- layer_out: bfloat16 [4096, 2560], P(('grp', 'tok'))
- new_latents: bfloat16 [4096, 288], P(('grp', 'tok'))
Inputs may be any that keep to these rules, and one draw needn't show every extreme that they name: `cache_len`: some request has exactly 4096 live cached rows. `prompt_len`: some stored prompt has exactly 1024 live rows. `cache_latents`: rows past a request's live length are stored but never read. `prompt_latents`: rows past a prompt's live length are stored but never read.
All inputs are finite; a program needn't handle non-finite values.
Results may differ from a plain program's by a relative error of at most 0.02.
Values may be sent and summed in bfloat16 or wider, within the bound.
A program may use at most 128 MiB of HBM per device.

v0:
```python
import jax
import jax.numpy as jnp
from jax import lax
from jax.sharding import PartitionSpec as P

KVR = 256
HEADS = 20
NOPE = 64
ROPE = 32
VDIM = 64
SPAN = 1024


EPSILON = 1e-06


def passed_along(block, axis, distance):
    devices = range(lax.axis_size(axis))
    route = [(i - distance, i) for i in devices if i - distance in devices]
    return lax.ppermute(block, axis, route)


def norm_rows(values, gain_vector):
    mean_square = jnp.mean(values * values, axis=-1, keepdims=True)
    return values * lax.rsqrt(mean_square + EPSILON) * gain_vector.astype(jnp.float32)


def rotate(values, positions):
    half_width = values.shape[-1] // 2
    frequency = 10000.0 ** (-jnp.arange(half_width, dtype=jnp.float32) / half_width)
    angles = positions.astype(jnp.float32)[:, None] * frequency[None, :]
    if values.ndim == 3:
        angles = angles[:, None, :]
    cosine = jnp.cos(angles)
    sine_part = jnp.sin(angles)
    leading = values[..., :half_width]
    trailing = values[..., half_width:]
    return jnp.concatenate(
        [leading * cosine - trailing * sine_part, trailing * cosine + leading * sine_part], axis=-1
    )


def attend_segment(
    softmax_state, queries, key_rows, lowers, limits, block_count, key_block, score_scale
):

    def fold_block(step_index, carried):
        running_max, running_sum, running_out = carried
        first_key = step_index * key_block
        key_piece = lax.dynamic_slice_in_dim(key_rows, first_key, key_block, 0)
        scores = (
            jnp.einsum("rw,kw->rk", queries, key_piece, preferred_element_type=jnp.float32)
            * score_scale
        )
        key_place = (first_key + jnp.arange(key_block, dtype=jnp.int32))[None, :]
        live_keys = jnp.logical_and(key_place >= lowers[:, None], key_place < limits[:, None])
        next_max = jnp.maximum(running_max, jnp.max(jnp.where(live_keys, scores, -1e30), axis=1))
        weights = jnp.where(live_keys, jnp.exp(scores - next_max[:, None]), 0.0)
        factor = jnp.exp(running_max - next_max)
        running_sum = running_sum * factor + jnp.sum(weights, axis=1)
        running_out = running_out * factor[:, None] + jnp.dot(
            weights.astype(jnp.bfloat16), key_piece[:, :KVR], preferred_element_type=jnp.float32
        )
        return (next_max, running_sum, running_out)

    return lax.fori_loop(0, block_count, fold_block, softmax_state)


def body(
    tokens,
    input_gain,
    query_down,
    query_gain,
    query_up,
    latent_down,
    latent_gain,
    key_up,
    value_up,
    output_weight,
    post_gain,
    gate_weight,
    up_weight,
    down_weight,
    cache_latents,
    prompt_latents,
    cache_len,
    prompt_len,
    prompt_of,
):
    group_index = lax.axis_index("grp")
    shard_index = lax.axis_index("tok")
    tok_dev = tokens.shape[0]
    tok_count = lax.axis_size("tok")
    group_requests = tok_dev * tok_count // SPAN
    local_request = shard_index % group_requests
    owner = group_index * group_requests + local_request
    offset = shard_index // group_requests * tok_dev
    within = offset + jnp.arange(tok_dev, dtype=jnp.int32)
    own_prompt = prompt_of[owner]
    prompt_live = prompt_len[own_prompt]
    cache_live = cache_len[owner]
    positions = prompt_live + cache_live + within
    normed = norm_rows(tokens.astype(jnp.float32), input_gain).astype(jnp.bfloat16)
    query_latent = norm_rows(
        jnp.dot(normed, query_down, preferred_element_type=jnp.float32), query_gain
    ).astype(jnp.bfloat16)
    query_full = jnp.dot(query_latent, query_up, preferred_element_type=jnp.float32).astype(
        jnp.bfloat16
    )
    query_full = lax.optimization_barrier(query_full).reshape(tok_dev, HEADS, NOPE + ROPE)
    absorbed = jnp.einsum(
        "thd,khd->thk",
        query_full[..., :NOPE],
        key_up.reshape(KVR, HEADS, NOPE),
        preferred_element_type=jnp.float32,
    )
    turned = rotate(query_full[..., NOPE:].astype(jnp.float32), positions)
    queries = jnp.concatenate([absorbed, turned], axis=-1).astype(jnp.bfloat16)
    latent_raw = jnp.dot(normed, latent_down, preferred_element_type=jnp.float32)
    new_latents = jnp.concatenate(
        [norm_rows(latent_raw[:, :KVR], latent_gain), rotate(latent_raw[:, KVR:], positions)],
        axis=-1,
    ).astype(jnp.bfloat16)
    latent_width = new_latents.shape[1]
    shards_back = SPAN // tok_dev
    earlier_pieces = []
    passing = new_latents
    for back in range(1, shards_back):
        passing = passed_along(passing, "tok", group_requests)
        earlier_pieces.insert(0, passing)
    span_rows = jnp.concatenate(earlier_pieces + [new_latents], axis=0)
    lead_rows = (shards_back - 1) * tok_dev
    span_lower = jnp.broadcast_to(lead_rows - offset, (tok_dev,))
    span_limit = lead_rows + 1 + jnp.arange(tok_dev, dtype=jnp.int32)
    cache_all, prompt_all = (
        lax.all_gather(cache_latents, "tok", axis=1, tiled=True),
        lax.all_gather(prompt_latents, "tok", axis=1, tiled=True),
    )
    cache_rows = lax.dynamic_index_in_dim(cache_all, local_request, 0, keepdims=False)
    prompt_rows = lax.dynamic_index_in_dim(prompt_all, own_prompt, 0, keepdims=False)
    query_rows = queries.reshape(tok_dev * HEADS, latent_width)
    row_count = tok_dev * HEADS
    score_scale = 1.0 / (NOPE + ROPE) ** 0.5
    softmax_state = (
        jnp.full((row_count,), -1e30, jnp.float32),
        jnp.zeros((row_count,), jnp.float32),
        jnp.zeros((row_count, KVR), jnp.float32),
    )
    no_lower = jnp.zeros((tok_dev,), jnp.int32)
    segments = (
        (prompt_rows, no_lower, jnp.broadcast_to(prompt_live, (tok_dev,))),
        (cache_rows, no_lower, jnp.broadcast_to(cache_live, (tok_dev,))),
        (span_rows, span_lower, span_limit),
    )
    for key_rows, token_lower, token_limit in segments:
        lowers = jnp.repeat(token_lower, HEADS)
        limits = jnp.repeat(token_limit, HEADS)
        key_block = min(512, key_rows.shape[0])
        block_count = key_rows.shape[0] // key_block
        softmax_state = attend_segment(
            softmax_state, query_rows, key_rows, lowers, limits, block_count, key_block, score_scale
        )
    running_max, running_sum, running_out = softmax_state
    latent_out = (
        (running_out / running_sum[:, None]).astype(jnp.bfloat16).reshape(tok_dev, HEADS, KVR)
    )
    heads_out = (
        jnp.einsum(
            "thk,khv->thv",
            latent_out,
            value_up.reshape(KVR, HEADS, VDIM),
            preferred_element_type=jnp.float32,
        )
        .astype(jnp.bfloat16)
        .reshape(tok_dev, HEADS * VDIM)
    )
    attended = jnp.dot(heads_out, output_weight, preferred_element_type=jnp.float32)
    residual = lax.optimization_barrier(
        (tokens.astype(jnp.float32) + attended).astype(jnp.bfloat16)
    )
    post_norm = norm_rows(residual.astype(jnp.float32), post_gain).astype(jnp.bfloat16)
    rows_all = lax.all_gather(post_norm, "grp", axis=0, tiled=True)
    gate_values = jnp.dot(
        rows_all,
        lax.all_gather(gate_weight, "tok", axis=0, tiled=True),
        preferred_element_type=jnp.float32,
    )
    up_values = jnp.dot(
        rows_all,
        lax.all_gather(up_weight, "tok", axis=0, tiled=True),
        preferred_element_type=jnp.float32,
    )
    hidden = (jax.nn.silu(gate_values) * up_values).astype(jnp.bfloat16)
    partial_out = jnp.dot(
        hidden,
        lax.all_gather(down_weight, "tok", axis=1, tiled=True),
        preferred_element_type=jnp.float32,
    )
    down_values = lax.psum_scatter(
        partial_out.astype(jnp.bfloat16), "grp", scatter_dimension=0, tiled=True
    ).astype(jnp.float32)
    layer_out = (residual.astype(jnp.float32) + down_values).astype(jnp.bfloat16)
    return (layer_out, new_latents)


def solution(mesh):
    in_specs = (
        P(("grp", "tok"), None),
        P(),
        P(),
        P(),
        P(),
        P(),
        P(),
        P(),
        P(),
        P(),
        P(),
        P("tok", "grp"),
        P("tok", "grp"),
        P("grp", "tok"),
        P("grp", "tok", None),
        P(None, "tok", None),
        P(),
        P(),
        P(),
    )
    out_specs = (P(("grp", "tok"), None), P(("grp", "tok"), None))
    return jax.shard_map(body, mesh=mesh, in_specs=in_specs, out_specs=out_specs, check_vma=False)
```

profile of v0, /device:TPU:8, one launch (start us, length us, event | category | flops | bytes accessed | tf_op | source)
XLA Modules:
  0.0 414.3 jit_solution(8707655572441244235)
XLA Ops:
  19.7 2.2 fusion.76
  24.2 3.1 multiply_reduce_fusion
  33.7 3.4 collective-permute-done.1
  37.1 5.9 %collective-permute-start.2 = (bf16[128,288]{0,1:T(8,128)(2,1)}, bf16[128,288]{0,1:T(8,128)(2,1)S(1)}, u32[]{:S(2)}, u32[]{:S(2)}) collective-permute-start(bf16[128,288]{0,1:T(8,128)(2,1)} %collective-permute-done.1), channel_id=1, source_target_pairs={{0,1},{1,2},{2,3},{3,4},{4,5},{5,6},{6,7},{8,9},{9,10},{10,11},{11... | collective-permute-start | bytes 221192 | tf_op jit(solution)/shard_map/ppermute | solution.py:20
  44.5 4.5 %collective-permute-start.3 = (bf16[128,288]{0,1:T(8,128)(2,1)S(1)}, bf16[128,288]{0,1:T(8,128)(2,1)S(1)}, u32[]{:S(2)}, u32[]{:S(2)}) collective-permute-start(bf16[128,288]{0,1:T(8,128)(2,1)S(1)} %collective-permute-done.2), channel_id=1, source_target_pairs={{0,1},{1,2},{2,3},{3,4},{4,5},{5,6},{6,7},{8,9},{9,10},{10,11},{11... | collective-permute-start | bytes 221192 | tf_op jit(solution)/shard_map/ppermute | solution.py:20
  49.1 2.6 collective-permute-done.3
  51.7 6.5 %collective-permute-start.4 = (bf16[128,288]{0,1:T(8,128)(2,1)S(1)}, bf16[128,288]{0,1:T(8,128)(2,1)S(1)}, u32[]{:S(2)}, u32[]{:S(2)}) collective-permute-start(bf16[128,288]{0,1:T(8,128)(2,1)S(1)} %collective-permute-done.3), channel_id=1, source_target_pairs={{0,1},{1,2},{2,3},{3,4},{4,5},{5,6},{6,7},{8,9},{9,10},{10,11},{11... | collective-permute-start | bytes 221192 | tf_op jit(solution)/shard_map/ppermute | solution.py:20
  63.9 4.4 %collective-permute-start.5 = (bf16[128,288]{0,1:T(8,128)(2,1)S(1)}, bf16[128,288]{0,1:T(8,128)(2,1)S(1)}, u32[]{:S(2)}, u32[]{:S(2)}) collective-permute-start(bf16[128,288]{0,1:T(8,128)(2,1)S(1)} %collective-permute-done.4), channel_id=1, source_target_pairs={{0,1},{1,2},{2,3},{3,4},{4,5},{5,6},{6,7},{8,9},{9,10},{10,11},{11... | collective-permute-start | bytes 221192 | tf_op jit(solution)/shard_map/ppermute | solution.py:20
  68.3 3.0 pad_maximum_fusion
  73.5 6.1 %collective-permute-start.6 = (bf16[128,288]{0,1:T(8,128)(2,1)S(1)}, bf16[128,288]{0,1:T(8,128)(2,1)S(1)}, u32[]{:S(2)}, u32[]{:S(2)}) collective-permute-start(bf16[128,288]{0,1:T(8,128)(2,1)S(1)} %collective-permute-done.5), channel_id=1, source_target_pairs={{0,1},{1,2},{2,3},{3,4},{4,5},{5,6},{6,7},{8,9},{9,10},{10,11},{11... | collective-permute-start | bytes 221192 | tf_op jit(solution)/shard_map/ppermute | solution.py:20
  90.0 26.7 %while.56 = (s32[]{:T(128)}, f32[2560]{0:T(1024)S(1)}, f32[2560]{0:T(1024)S(1)}, f32[2560,256]{1,0:T(8,128)S(1)}, bf16[1024,288]{1,0:T(8,128)(2,1)}, /*index=5*/...) while((s32[]{:T(128)}, f32[2560]{0:T(1024)S(1)}, ...), condition=%wide.region_5.6_spmd.clone, body=%wide.region_2.5_spmd.clone.sunk | while | flops 1439840768 | bytes 44730576 | solution.py:66
  90.6 5.6 %fusion.130 = (f32[2560]{0:T(1024)S(1)}, f32[512,2560]{1,0:T(8,128)}) fusion(pred[512]{0:T(512)(128)(4,1)S(1)} %fusion.129, bf16[2560,288]{1,0:T(8,128)(2,1)} %get-tuple-element.733, bf16[1024,288]{1,0:T(8,128)(2,1)} %get-tuple-element.732, s32[]{:T(128)S(6)} %select_n.143), kind=kOutput, calls=%fused_computation.53.clone.1 | convolution fusion | flops 758904320 | bytes 7612932 | tf_op jit(solution)/shard_map/while/body/eval_jaxpr/rw,kw->rk/dot_general | solution.py:52
  96.2 3.6 fusion.131
  100.3 2.9 convolution_add_fusion.9
  103.8 5.6 %fusion.130 = (f32[2560]{0:T(1024)S(1)}, f32[512,2560]{1,0:T(8,128)}) fusion(pred[512]{0:T(512)(128)(4,1)S(1)} %fusion.129, bf16[2560,288]{1,0:T(8,128)(2,1)} %get-tuple-element.733, bf16[1024,288]{1,0:T(8,128)(2,1)} %get-tuple-element.732, s32[]{:T(128)S(6)} %select_n.143), kind=kOutput, calls=%fused_computation.53.clone.1 | convolution fusion | flops 758904320 | bytes 7612932 | tf_op jit(solution)/shard_map/while/body/eval_jaxpr/rw,kw->rk/dot_general | solution.py:52
  109.4 3.5 fusion.131
  113.7 2.9 convolution_add_fusion.9
  116.7 61.4 %while.54 = (s32[]{:T(128)}, f32[2560]{0:T(1024)S(1)}, f32[2560]{0:T(1024)S(1)}, f32[2560,256]{1,0:T(8,128)S(1)}, bf16[4096,288]{1,0:T(8,128)(2,1)}, /*index=5*/...) while((s32[]{:T(128)}, f32[2560]{0:T(1024)S(1)}, ...), condition=%wide.region_9.10_spmd.clone, body=%wide.region_6.9_spmd.clone.sunk | while | flops 1439177728 | bytes 23759020 | solution.py:66
  117.3 3.3 fusion.119
  121.6 2.7 convolution_add_fusion.7
  124.9 3.4 fusion.119
  129.4 2.7 convolution_add_fusion.7
  132.7 3.3 fusion.119
  137.0 2.7 convolution_add_fusion.7
  140.3 3.4 fusion.119
  144.8 2.7 convolution_add_fusion.7
  148.0 3.3 fusion.119
  152.4 2.7 convolution_add_fusion.7
  155.7 3.3 fusion.119
  160.1 2.7 convolution_add_fusion.7
  163.4 3.3 fusion.119
  167.8 2.7 convolution_add_fusion.7
  171.0 3.3 fusion.119
  175.4 2.7 convolution_add_fusion.7
  178.1 19.2 %while.55 = (s32[]{:T(128)}, f32[2560]{0:T(1024)S(1)}, f32[2560]{0:T(1024)S(1)}, f32[2560,256]{1,0:T(8,128)S(1)}, bf16[1024,288]{0,1:T(8,128)(2,1)}, /*index=5*/...) while((s32[]{:T(128)}, f32[2560]{0:T(1024)S(1)}, ...), condition=%wide.region_14.15_spmd.clone, body=%wide.region_11.14_spmd.clone.sunk | while | flops 1447041536 | bytes 23730872 | solution.py:66
  178.6 4.0 fusion.124
  184.5 3.3 convolution_add_fusion.8
  188.0 4.0 fusion.124
  194.0 3.3 convolution_add_fusion.8
  198.8 2.3 reshape.148
  201.7 3.9 fusion.59
  208.5 43.2 %all-gather.11.cloned.1.call-done = bf16[512,2560]{1,0:T(8,128)(2,1)} async-done(((bf16[128,2560]{1,0:T(8,128)(2,1)}), bf16[512,2560]{1,0:T(8,128)(2,1)}) %all-gather.11.cloned.1.call-update) | async-done | bytes 2621456 | tf_op jit(solution)/shard_map/all_gather | solution.py:182
  251.7 6.7 %fusion.81 = f32[512,800]{0,1:T(8,128)} fusion(bf16[512,2560]{1,0:T(8,128)(2,1)} %all-gather.11.cloned.1.call-done, bf16[2560,800]{1,0:T(8,128)(2,1)} %all-gather.13.cloned.1.call-done), kind=kOutput, calls=%fused_computation.135 | convolution fusion | flops 2097152000 | bytes 8355840 | tf_op jit(solution)/shard_map/dot_general | solution.py:183
  258.4 44.0 %all-gather.15.cloned.1.call-done = bf16[2560,800]{1,0:T(8,128)(2,1)} async-done(((bf16[320,800]{1,0:T(8,128)(2,1)}), bf16[2560,800]{1,0:T(8,128)(2,1)}) %all-gather.15.cloned.1.call-update) | async-done | bytes 4096016 | tf_op jit(solution)/shard_map/all_gather | solution.py:190
  302.3 51.0 %all-gather.17.cloned.1.call-done = bf16[800,2560]{0,1:T(8,128)(2,1)} async-done(((bf16[800,320]{0,1:T(8,128)(2,1)}), bf16[800,2560]{0,1:T(8,128)(2,1)}) %all-gather.17.cloned.1.call-update) | async-done | bytes 4096016 | tf_op jit(solution)/shard_map/all_gather | solution.py:196
  353.3 11.8 %convolution_convert_fusion = bf16[512,2560]{1,0:T(8,128)(2,1)} fusion(bf16[800,2560]{0,1:T(8,128)(2,1)} %all-gather.17.cloned.1.call-done, f32[512,800]{0,1:T(8,128)} %fusion.81, bf16[512,2560]{1,0:T(8,128)(2,1)} %all-gather.11.cloned.1.call-done, bf16[2560,800]{1,0:T(8,128)(2,1)} %all-gather.15.cloned.1.call-done), kind=kOutput, calls=%fused_computation.77 | convolution fusion | flops 4198072320 | bytes 15073280 | tf_op jit(solution)/shard_map/dot_general | solution.py:194
  365.2 40.0 %reduce-scatter.2.cloned.1.call-done = bf16[128,2560]{1,0:T(8,128)(2,1)} async-done(((bf16[512,2560]{1,0:T(8,128)(2,1)}), bf16[128,2560]{1,0:T(8,128)(2,1)}) %reduce-scatter.2.cloned.1.call-update) | async-done | bytes 655376 | tf_op jit(solution)/shard_map/reduce_scatter | solution.py:199
  405.2 2.3 fusion.67
  (160 shorter events, 62.0 us)
Async XLA Ops:
  7.2 24.3 %copy-start = (bf16[768,1920]{1,0:T(8,128)(2,1)S(1)}, bf16[768,1920]{1,0:T(8,128)(2,1)}, u32[]{:S(2)}) copy-start(bf16[768,1920]{1,0:T(8,128)(2,1)} %param.29) | copy-start | bytes 8847364
  7.2 80.5 %all-gather.7.cloned.1.call-start = ((), (), s32[]{:S(2)}) async-start(), calls=%async_computation.1 | async-start | bytes 5308416 | tf_op jit(solution)/shard_map/all_gather | solution.py:137
  7.9 108.8 %all-gather.9.cloned.1.call-start = ((), (), s32[]{:S(2)}) async-start(), calls=%async_computation.2 | async-start | bytes 3538944 | tf_op jit(solution)/shard_map/all_gather | solution.py:136
  10.0 198.5 %all-gather.13.cloned.1.call-start = ((), (), s32[]{:S(2)}) async-start(), calls=%async_computation.4 | async-start | bytes 5160960 | tf_op jit(solution)/shard_map/all_gather | solution.py:185
  22.2 5.2 %copy-start.6 = (bf16[128,288]{0,1:T(8,128)(2,1)}, bf16[128,288]{0,1:T(8,128)(2,1)S(1)}, u32[]{:S(2)}) copy-start(bf16[128,288]{0,1:T(8,128)(2,1)S(1)} %pad_maximum_fusion.1) | copy-start | bytes 221188
  22.2 7.3 %collective-permute-start = (bf16[128,288]{0,1:T(8,128)(2,1)S(1)}, bf16[128,288]{0,1:T(8,128)(2,1)}, u32[]{:S(2)}, u32[]{:S(2)}) collective-permute-start(bf16[128,288]{0,1:T(8,128)(2,1)S(1)} %pad_maximum_fusion.1), channel_id=1, source_target_pairs={{0,1},{1,2},{2,3},{3,4},{4,5},{5,6},{6,7},{8,9},{9,10},{10,11},{11... | collective-permute-start | bytes 221192 | tf_op jit(solution)/shard_map/ppermute | solution.py:20
  24.2 3.2 copy-start.8
  24.2 227.5 %all-gather.11.cloned.1.call-start = ((), (), s32[]{:S(2)}) async-start(), calls=%async_computation.3 | async-start | bytes 3276800 | tf_op jit(solution)/shard_map/all_gather | solution.py:182
  29.5 7.5 %collective-permute-start.1 = (bf16[128,288]{0,1:T(8,128)(2,1)}, bf16[128,288]{0,1:T(8,128)(2,1)}, u32[]{:S(2)}, u32[]{:S(2)}) collective-permute-start(bf16[128,288]{0,1:T(8,128)(2,1)} %collective-permute-done), channel_id=1, source_target_pairs={{0,1},{1,2},{2,3},{3,4},{4,5},{5,6},{6,7},{8,9},{9,10},{10,11},{11... | collective-permute-start | bytes 221192 | tf_op jit(solution)/shard_map/ppermute | solution.py:20
  37.1 7.4 %collective-permute-start.2 = (bf16[128,288]{0,1:T(8,128)(2,1)}, bf16[128,288]{0,1:T(8,128)(2,1)S(1)}, u32[]{:S(2)}, u32[]{:S(2)}) collective-permute-start(bf16[128,288]{0,1:T(8,128)(2,1)} %collective-permute-done.1), channel_id=1, source_target_pairs={{0,1},{1,2},{2,3},{3,4},{4,5},{5,6},{6,7},{8,9},{9,10},{10,11},{11... | collective-permute-start | bytes 221192 | tf_op jit(solution)/shard_map/ppermute | solution.py:20
  44.5 7.2 %collective-permute-start.3 = (bf16[128,288]{0,1:T(8,128)(2,1)S(1)}, bf16[128,288]{0,1:T(8,128)(2,1)S(1)}, u32[]{:S(2)}, u32[]{:S(2)}) collective-permute-start(bf16[128,288]{0,1:T(8,128)(2,1)S(1)} %collective-permute-done.2), channel_id=1, source_target_pairs={{0,1},{1,2},{2,3},{3,4},{4,5},{5,6},{6,7},{8,9},{9,10},{10,11},{11... | collective-permute-start | bytes 221192 | tf_op jit(solution)/shard_map/ppermute | solution.py:20
  51.7 12.2 %collective-permute-start.4 = (bf16[128,288]{0,1:T(8,128)(2,1)S(1)}, bf16[128,288]{0,1:T(8,128)(2,1)S(1)}, u32[]{:S(2)}, u32[]{:S(2)}) collective-permute-start(bf16[128,288]{0,1:T(8,128)(2,1)S(1)} %collective-permute-done.3), channel_id=1, source_target_pairs={{0,1},{1,2},{2,3},{3,4},{4,5},{5,6},{6,7},{8,9},{9,10},{10,11},{11... | collective-permute-start | bytes 221192 | tf_op jit(solution)/shard_map/ppermute | solution.py:20
  63.9 9.6 %copy-start.7 = (bf16[2560]{0:T(1024)(128)(2,1)S(1)}, bf16[2560]{0:T(1024)(128)(2,1)}, u32[]{:S(2)}) copy-start(bf16[2560]{0:T(1024)(128)(2,1)} %param.35) | copy-start | bytes 15364
  63.9 9.6 %collective-permute-start.5 = (bf16[128,288]{0,1:T(8,128)(2,1)S(1)}, bf16[128,288]{0,1:T(8,128)(2,1)S(1)}, u32[]{:S(2)}, u32[]{:S(2)}) collective-permute-start(bf16[128,288]{0,1:T(8,128)(2,1)S(1)} %collective-permute-done.4), channel_id=1, source_target_pairs={{0,1},{1,2},{2,3},{3,4},{4,5},{5,6},{6,7},{8,9},{9,10},{10,11},{11... | collective-permute-start | bytes 221192 | tf_op jit(solution)/shard_map/ppermute | solution.py:20
  73.5 7.2 %collective-permute-start.6 = (bf16[128,288]{0,1:T(8,128)(2,1)S(1)}, bf16[128,288]{0,1:T(8,128)(2,1)S(1)}, u32[]{:S(2)}, u32[]{:S(2)}) collective-permute-start(bf16[128,288]{0,1:T(8,128)(2,1)S(1)} %collective-permute-done.5), channel_id=1, source_target_pairs={{0,1},{1,2},{2,3},{3,4},{4,5},{5,6},{6,7},{8,9},{9,10},{10,11},{11... | collective-permute-start | bytes 221192 | tf_op jit(solution)/shard_map/ppermute | solution.py:20
  96.2 4.1 copy-start.2
  109.4 4.3 %copy-start.2 = (f32[512,2560]{1,0:T(8,128)S(1)}, f32[512,2560]{1,0:T(8,128)}, u32[]{:S(2)}) copy-start(f32[512,2560]{1,0:T(8,128)} %get-tuple-element.703) | copy-start | bytes 15728644 | tf_op jit(solution)/shard_map/while
  198.8 2.3 copy-start.5
  198.8 2.9 copy-start.4
  205.6 52.7 %copy-start.3 = (bf16[128,2560]{1,0:T(8,128)(2,1)}, bf16[128,2560]{1,0:T(8,128)(2,1)S(1)}, u32[]{:S(2)}) copy-start(bf16[128,2560]{1,0:T(8,128)(2,1)S(1)} %fusion.59) | copy-start | bytes 1966084
  207.0 95.4 %all-gather.15.cloned.1.call-start = ((), (), s32[]{:S(2)}) async-start(), calls=%async_computation.5 | async-start | bytes 5160960 | tf_op jit(solution)/shard_map/all_gather | solution.py:190
  207.6 145.8 %all-gather.17.cloned.1.call-start = ((), (), s32[]{:S(2)}) async-start(), calls=%async_computation.6 | async-start | bytes 5160960 | tf_op jit(solution)/shard_map/all_gather | solution.py:196
  208.1 197.1 %reduce-scatter.2.cloned.1.call-start = ((), (), s32[]{:S(2)}) async-start(), calls=%async_computation.7 | async-start | bytes 3276800 | tf_op jit(solution)/shard_map/reduce_scatter | solution.py:199
  353.3 54.1 %copy-start.1 = (bf16[768,1920]{1,0:T(8,128)(2,1)S(1)}, bf16[768,1920]{1,0:T(8,128)(2,1)}, u32[]{:S(2)}) copy-start(bf16[768,1920]{1,0:T(8,128)(2,1)} %param.29) | copy-start | bytes 8847364
Sparse Core Ops, SparseCore 0:
  9.6 54.1 all-gather.6
  65.5 37.6 all-gather.8
  104.9 49.7 all-gather.12
  207.1 44.5 all-gather.10
  253.2 49.1 all-gather.14
  303.8 49.4 all-gather.16
  365.3 39.8 reduce-scatter.1
where the time goes:
time: 418 us; the launch traced here: 414 us
  waiting for transfers between devices  190 us (45%)
  matrix products  109 us (26%)
  other arithmetic  36.9 us (9%)
  starting transfers between devices  31.8 us (8%)
  local copies, waits for them, and re-layouts  27.6 us (7%)
  between operations  17.6 us (4%)
    all_gather x1, waiting for transfers between devices, body(): lax.all_gather(down_weight, 'tok', axis=1, tiled=True)  51 us
    dot_general x12, matrix products, fold_block(): jnp.einsum('rw,kw->rk', queries, key_piece, preferred_element_type=jnp.fl...  45.9 us
    all_gather x1, waiting for transfers between devices, body(): lax.all_gather(up_weight, 'tok', axis=0, tiled=True)  44 us
    all_gather x1, waiting for transfers between devices, body(): rows_all = lax.all_gather(post_norm, 'grp', axis=0, tiled=True)  43.2 us
    reduce_scatter x1, waiting for transfers between devices, body(): lax.psum_scatter(partial_out.astype(jnp.bfloat16), 'grp', scatter_dimensi...  40 us
    dot_general x12, matrix products, fold_block(): jnp.dot(weights.astype(jnp.bfloat16), key_piece[:, :KVR], preferred_eleme...  33.7 us
    ppermute x7, starting transfers between devices, passed_along(): return lax.ppermute(block, axis, route)  31.2 us
    reduce_sum x12, other arithmetic, fold_block(): running_sum = running_sum * factor + jnp.sum(weights, axis=1)  19 us
  transfers between devices with their start and end apart: 14, of which 9 were waited for; matrix products, arithmetic and copies ran while one was open for 38% of the time, Pallas kernels for 0%

commit v1 on v0

v1 whole, which is shorter than its diff:
```python
import functools

import jax
import jax.numpy as jnp
from jax import lax
from jax.experimental import pallas as pl
from jax.experimental.pallas import tpu as pltpu
from jax.sharding import PartitionSpec as P

KVR = 256
HEADS = 20
NOPE = 64
ROPE = 32
VDIM = 64
SPAN = 1024
MARK = 384


EPSILON = 1e-06


def norm_rows(values, gain_vector):
    mean_square = jnp.mean(values * values, axis=-1, keepdims=True)
    return values * lax.rsqrt(mean_square + EPSILON) * gain_vector.astype(jnp.float32)


def rotate(values, positions):
    half_width = values.shape[-1] // 2
    frequency = 10000.0 ** (-jnp.arange(half_width, dtype=jnp.float32) / half_width)
    angles = positions.astype(jnp.float32)[:, None] * frequency[None, :]
    if values.ndim == 3:
        angles = angles[:, None, :]
    cosine = jnp.cos(angles)
    sine_part = jnp.sin(angles)
    leading = values[..., :half_width]
    trailing = values[..., half_width:]
    return jnp.concatenate(
        [leading * cosine - trailing * sine_part, trailing * cosine + leading * sine_part], axis=-1
    )


def flash_kernel(row_block, key_block, q_ref, prompt_ref, cache_ref, span_ref, out_ref):
    segments = []
    for ref in (prompt_ref, cache_ref, span_ref):
        for first in range(0, ref.shape[0], key_block):
            segments.append(ref.at[pl.ds(first, min(key_block, ref.shape[0]))])

    @pl.loop(0, q_ref.shape[0] // row_block)
    def _(step):
        rows = pl.ds(pl.multiple_of(step * row_block, row_block), row_block)
        q = q_ref[rows, :]

        def score(keys):
            return lax.dot_general(
                q, keys[...], (((1,), (1,)), ((), ())), preferred_element_type=jnp.float32
            )

        scores = score(segments[0])
        largest = None
        for at, keys in enumerate(segments):
            following = score(segments[at + 1]) if at + 1 < len(segments) else None
            block_max = jnp.max(scores, axis=1, keepdims=True)
            new_max = block_max if at == 0 else jnp.maximum(largest, block_max)
            weights = jnp.exp2(scores - new_max)
            block_sum = jnp.sum(weights, axis=1, keepdims=True)
            product = jnp.dot(
                weights.astype(jnp.bfloat16), keys[:, :KVR], preferred_element_type=jnp.float32
            )
            if at == 0:
                total, mixed = block_sum, product
            else:
                factor = jnp.exp2(largest - new_max)
                total = total * factor + block_sum
                mixed = mixed * factor + product
            largest, scores = new_max, following
        out_ref[rows, :] = (mixed / total).astype(jnp.bfloat16)


def flash(queries, prompt_keys, cache_keys, span_keys):
    rows = queries.shape[0]
    count = prompt_keys.shape[0] + cache_keys.shape[0] + span_keys.shape[0]
    return pl.pallas_call(
        functools.partial(flash_kernel, 512, 512),
        out_shape=jax.ShapeDtypeStruct((rows, KVR), jnp.bfloat16),
        in_specs=[pl.BlockSpec(memory_space=pltpu.VMEM)] * 4,
        out_specs=pl.BlockSpec(memory_space=pltpu.VMEM),
        cost_estimate=pl.CostEstimate(
            flops=2 * rows * count * 768, bytes_accessed=2**24, transcendentals=rows * count
        ),
        compiler_params=pltpu.CompilerParams(vmem_limit_bytes=48 * 2**20),
    )(queries, prompt_keys, cache_keys, span_keys)


def widened(key_rows, live, hidden_at):
    rows = jnp.where(live[:, None], key_rows, jnp.zeros_like(key_rows))
    bias = jnp.where(live, 0.0, -1e30).astype(jnp.bfloat16)[:, None]
    between = jnp.zeros((rows.shape[0], MARK - rows.shape[1] - 1), jnp.bfloat16)
    return jnp.concatenate([rows, bias, between, hidden_at], axis=1)


def body(
    tokens,
    input_gain,
    query_down,
    query_gain,
    query_up,
    latent_down,
    latent_gain,
    key_up,
    value_up,
    output_weight,
    post_gain,
    gate_weight,
    up_weight,
    down_weight,
    cache_latents,
    prompt_latents,
    cache_len,
    prompt_len,
    prompt_of,
):
    group_index = lax.axis_index("grp")
    shard_index = lax.axis_index("tok")
    tok_dev = tokens.shape[0]
    tok_count = lax.axis_size("tok")
    group_requests = tok_dev * tok_count // SPAN
    local_request = shard_index % group_requests
    owner = group_index * group_requests + local_request
    offset = shard_index // group_requests * tok_dev
    within = offset + jnp.arange(tok_dev, dtype=jnp.int32)
    own_prompt = prompt_of[owner]
    prompt_live = prompt_len[own_prompt]
    cache_live = cache_len[owner]
    positions = prompt_live + cache_live + within
    normed = norm_rows(tokens.astype(jnp.float32), input_gain).astype(jnp.bfloat16)
    query_latent = norm_rows(
        jnp.dot(normed, query_down, preferred_element_type=jnp.float32), query_gain
    ).astype(jnp.bfloat16)
    query_full = jnp.dot(query_latent, query_up, preferred_element_type=jnp.float32).astype(
        jnp.bfloat16
    )
    query_full = lax.optimization_barrier(query_full).reshape(tok_dev, HEADS, NOPE + ROPE)
    score_scale = 1.4426950408889634 / (NOPE + ROPE) ** 0.5
    absorbed = jnp.einsum(
        "thd,khd->htk",
        query_full[..., :NOPE],
        key_up.reshape(KVR, HEADS, NOPE),
        preferred_element_type=jnp.float32,
    )
    turned = rotate(query_full[..., NOPE:].astype(jnp.float32), positions).transpose(1, 0, 2)
    queries = (jnp.concatenate([absorbed, turned], axis=-1) * score_scale).astype(jnp.bfloat16)
    marks = jnp.concatenate(
        [
            jnp.ones((tok_dev, 1), jnp.bfloat16),
            jnp.zeros((tok_dev, MARK - KVR - ROPE - 1), jnp.bfloat16),
            jnp.eye(tok_dev, dtype=jnp.bfloat16),
        ],
        axis=1,
    )
    query_rows = jnp.concatenate(
        [queries, jnp.broadcast_to(marks, (HEADS,) + marks.shape)], axis=-1
    ).reshape(HEADS * tok_dev, MARK + tok_dev)
    latent_raw = jnp.dot(normed, latent_down, preferred_element_type=jnp.float32)
    new_latents = jnp.concatenate(
        [norm_rows(latent_raw[:, :KVR], latent_gain), rotate(latent_raw[:, KVR:], positions)],
        axis=-1,
    ).astype(jnp.bfloat16)
    group_prompts = jnp.concatenate(
        [
            lax.dynamic_slice_in_dim(
                prompt_latents, prompt_of[group_index * group_requests + each], 1, 0
            )
            for each in range(group_requests)
        ],
        axis=0,
    )
    cache_all = lax.all_gather(cache_latents, "tok", axis=1, tiled=True)
    prompt_all = lax.all_gather(group_prompts, "tok", axis=1, tiled=True)
    span_all = lax.all_gather(new_latents, "tok", axis=0)
    cache_rows = lax.dynamic_index_in_dim(cache_all, local_request, 0, keepdims=False)
    prompt_rows = lax.dynamic_index_in_dim(prompt_all, local_request, 0, keepdims=False)
    span_rows = lax.dynamic_index_in_dim(
        span_all.reshape(SPAN // tok_dev, group_requests, tok_dev, KVR + ROPE),
        local_request,
        1,
        keepdims=False,
    ).reshape(SPAN, KVR + ROPE)
    span_place = jnp.arange(SPAN, dtype=jnp.int32)
    hidden = jnp.where(span_place[:, None] <= within[None, :], 0.0, -1e30).astype(jnp.bfloat16)
    prompt_live_rows = jnp.arange(prompt_rows.shape[0], dtype=jnp.int32) < prompt_live
    cache_live_rows = jnp.arange(cache_rows.shape[0], dtype=jnp.int32) < cache_live
    latent_out = flash(
        query_rows,
        widened(
            prompt_rows,
            prompt_live_rows,
            jnp.zeros((prompt_rows.shape[0], tok_dev), jnp.bfloat16),
        ),
        widened(
            cache_rows, cache_live_rows, jnp.zeros((cache_rows.shape[0], tok_dev), jnp.bfloat16)
        ),
        widened(span_rows, span_place >= 0, hidden),
    ).reshape(HEADS, tok_dev, KVR)
    heads_out = (
        jnp.einsum(
            "htk,khv->thv",
            latent_out,
            value_up.reshape(KVR, HEADS, VDIM),
            preferred_element_type=jnp.float32,
        )
        .astype(jnp.bfloat16)
        .reshape(tok_dev, HEADS * VDIM)
    )
    attended = jnp.dot(heads_out, output_weight, preferred_element_type=jnp.float32)
    residual = lax.optimization_barrier(
        (tokens.astype(jnp.float32) + attended).astype(jnp.bfloat16)
    )
    post_norm = norm_rows(residual.astype(jnp.float32), post_gain).astype(jnp.bfloat16)
    rows_all = lax.all_gather(post_norm, "grp", axis=0, tiled=True)
    gate_values = jnp.dot(
        rows_all,
        lax.all_gather(gate_weight, "tok", axis=0, tiled=True),
        preferred_element_type=jnp.float32,
    )
    up_values = jnp.dot(
        rows_all,
        lax.all_gather(up_weight, "tok", axis=0, tiled=True),
        preferred_element_type=jnp.float32,
    )
    hidden = (jax.nn.silu(gate_values) * up_values).astype(jnp.bfloat16)
    partial_out = jnp.dot(
        hidden,
        lax.all_gather(down_weight, "tok", axis=1, tiled=True),
        preferred_element_type=jnp.float32,
    )
    down_values = lax.psum_scatter(
        partial_out.astype(jnp.bfloat16), "grp", scatter_dimension=0, tiled=True
    ).astype(jnp.float32)
    layer_out = (residual.astype(jnp.float32) + down_values).astype(jnp.bfloat16)
    return (layer_out, new_latents)


def solution(mesh):
    in_specs = (
        P(("grp", "tok"), None),
        P(),
        P(),
        P(),
        P(),
        P(),
        P(),
        P(),
        P(),
        P(),
        P(),
        P("tok", "grp"),
        P("tok", "grp"),
        P("grp", "tok"),
        P("grp", "tok", None),
        P(None, "tok", None),
        P(),
        P(),
        P(),
    )
    out_specs = (P(("grp", "tok"), None), P(("grp", "tok"), None))
    return jax.shard_map(body, mesh=mesh, in_specs=in_specs, out_specs=out_specs, check_vma=False)
```

time: 418 us -> 332 us (0.79)
  matrix products: 109 us -> 26.6 us
  blocking collectives: 0 us -> 37 us
  starting transfers between devices: 31.8 us -> 0.46 us
  Pallas kernels: 0 us -> 31.3 us
  waiting for transfers between devices: 190 us -> 176 us
  local copies, waits for them, and re-layouts: 27.6 us -> 15.5 us
  other arithmetic: 36.9 us -> 25.6 us
    dot_general x26 -> x2, matrix products: 80.8 us -> 2.4 us  [the longest x1 1.83 us: body(): jnp.einsum('thd,khd->htk', query_full[..., :NOPE], key_up.reshape(KVR, HE...]
    all_gather x0 -> x2, blocking collectives: none -> 37 us  [the longest x1 19.5 us: body(): prompt_all = lax.all_gather(group_prompts, 'tok', axis=1, tiled=True)]
    pallas_call x0 -> x1, Pallas kernels: none -> 31.3 us  [flash(): pl.pallas_call(functools.partial(flash_kernel, 512, 512), out_shape=jax.S...]
    ppermute x7 -> x0, starting transfers between devices: 31.2 us -> none  [passed_along(): return lax.ppermute(block, axis, route)]
    reduce_sum x12 -> x0, other arithmetic: 19 us -> none  [fold_block(): running_sum = running_sum * factor + jnp.sum(weights, axis=1)]
    ppermute x7 -> x0, waiting for transfers between devices: 10.2 us -> none  [passed_along(): return lax.ppermute(block, axis, route)]
    and x10 -> x0, other arithmetic: 5.76 us -> none  [fold_block(): jnp.logical_and(key_place >= lowers[:, None], key_place < limits[:, None])]
    convert_element_type x2 -> x6, other arithmetic: 1.55 us -> 5.91 us  [the longest x2 3.33 us: widened(): bias = jnp.where(live, 0.0, -1e+30).astype(jnp.bfloat16)[:, None]]
  transfers between devices with their start and end apart: 14 -> 6, of which waited for: 9 -> 4; matrix products, arithmetic and copies ran while one was open for 38% -> 15% of each run, Pallas kernels for 0% -> 9%
where the time goes in v1:
time: 332 us; the launch traced here: 330 us
  waiting for transfers between devices  176 us (53%)
  blocking collectives  37 us (11%)
  Pallas kernels  31.3 us (9%)
  matrix products  26.6 us (8%)
  other arithmetic  25.6 us (8%)
  between operations  17.7 us (5%)
  local copies, waits for them, and re-layouts  15.5 us (5%)
    all_gather x1, waiting for transfers between devices, body(): lax.all_gather(down_weight, 'tok', axis=1, tiled=True)  51 us
    all_gather x1, waiting for transfers between devices, body(): lax.all_gather(up_weight, 'tok', axis=0, tiled=True)  45.2 us
    all_gather x1, waiting for transfers between devices, body(): rows_all = lax.all_gather(post_norm, 'grp', axis=0, tiled=True)  39.5 us
    reduce_scatter x1, waiting for transfers between devices, body(): lax.psum_scatter(partial_out.astype(jnp.bfloat16), 'grp', scatter_dimensi...  38.4 us
    pallas_call x1, Pallas kernels, flash(): pl.pallas_call(functools.partial(flash_kernel, 512, 512), out_shape=jax.S...  31.3 us
    all_gather x1, blocking collectives, body(): prompt_all = lax.all_gather(group_prompts, 'tok', axis=1, tiled=True)  19.5 us
    all_gather x1, blocking collectives, body(): span_all = lax.all_gather(new_latents, 'tok', axis=0)  17.4 us
    dot_general x1, matrix products, body(): jnp.dot(hidden, lax.all_gather(down_weight, 'tok', axis=1, tiled=True), p...  11.2 us
  transfers between devices with their start and end apart: 6, of which 4 were waited for; matrix products, arithmetic and copies ran while one was open for 15% of the time, Pallas kernels for 9%

profile of v1, /device:TPU:8, one launch (start us, length us, event | category | flops | bytes accessed | tf_op | source)
XLA Modules:
  0.0 330.1 jit_solution(15936986535924366425)
XLA Ops:
  7.2 2.0 copy.41
  9.3 0.7 all-gather.10.cloned.1.call-update
  10.1 0.6 fusion.17
  10.7 1.2 dynamic_slice.19
  13.9 1.2 dynamic_slice.20
  15.1 1.2 iota_compare_fusion.5
  16.3 1.4 select_convert_fusion.2
  17.8 1.2 dynamic_slice.21
  20.3 0.5 iota_add_fusion
  20.8 0.7 convert_element_type.106
  21.5 1.3 fusion.2
  22.8 2.9 fusion.13
  25.7 3.0 multiply_reduce_fusion
  28.7 0.6 convolution_convert_fusion.1
  29.7 1.1 multiply_reduce_fusion.1
  30.8 0.8 subtract_convert_fusion
  31.7 1.6 copy.39
  33.3 1.1 copy.38
  34.4 1.8 fusion.9
  36.4 17.4 %all_gather.24 = bf16[8,128,288]{1,2,0:T(8,128)(2,1)S(1)} all-gather(bf16[1,128,288]{1,2,0:T(8,128)(2,1)S(1)} %pad_maximum_fusion.2), channel_id=1, replica_groups=mesh['grp'=4,'tok'=8] {'tok'}, dimensions={0}, use_global_device_ids=true | all-gather | bytes 663552 | tf_op jit(solution)/shard_map/all_gather | solution.py:179
  53.8 1.2 copy.42
  55.0 0.9 constant_dynamic-slice_fusion
  56.0 19.5 %all_gather.22 = bf16[1,1024,288]{2,1,0:T(8,128)(2,1)} all-gather(bf16[1,128,288]{2,1,0:T(8,128)(2,1)S(1)} %copy.44), channel_id=1, replica_groups=mesh['grp'=4,'tok'=8] {'tok'}, dimensions={1}, use_global_device_ids=true | all-gather | bytes 663552 | tf_op jit(solution)/shard_map/all_gather | solution.py:178
  75.8 2.2 copy.43
  78.0 1.9 fusion
  80.3 0.8 copy-done.8
  81.0 1.8 pad_maximum_fusion.1
  82.9 0.6 iota_compare_fusion.4
  83.6 0.8 pad_maximum_fusion.q_ref
  84.4 1.9 select_convert_fusion
  86.3 2.4 bitcast_select_fusion
  88.7 3.5 %maximum_maximum_fusion.cache_ref = bf16[4096,512]{1,0:T(8,128)(2,1)} fusion(bf16[4096,1]{1,0:T(8,128)(2,1)S(1)} %copy-done.7, bf16[4096,288]{1,0:T(8,128)(2,1)S(1)} %bitcast_select_fusion, bf16[512]{0:T(512)(128)(2,1)S(1)} %pad.17.clone, bf16[512]{0:T(512)(128)(2,1)S(1)} %pad.16.clone), kind=kLoop, calls=%fused_computation.1 | loop fusion | flops 16777216 | bytes 6563840 | tf_op jit(solution)/shard_map/concatenate | solution.py:98
  92.3 31.3 %shard_map.194 = bf16[2560,256]{1,0:T(8,128)(2,1)S(1)} custom-call(bf16[2560,512]{1,0:T(8,128)(2,1)S(1)} %pad_maximum_fusion.q_ref, bf16[1024,512]{1,0:T(8,128)(2,1)S(1)} %copy-done.3, bf16[4096,512]{1,0:T(8,128)(2,1)} %maximum_maximum_fusion.cache_ref, bf16[1024,512]{1,0:T(8,128)(2,1)S(1)} %copy-done.2), custom_call_target="tpu_custom_call" | custom-call | flops 24159191040 | bytes 16777216 | tf_op jit(solution)/shard_map/pallas_call | solution.py:82
  123.6 0.6 convolution_convert_fusion.2
  124.2 0.5 copy-done.6
  124.7 1.0 fusion.1
  126.0 1.1 fusion.7
  127.1 0.5 all-gather.12.cloned.1.call-update
  127.7 0.5 all-gather.14.cloned.1.call-update
  128.6 39.5 %all-gather.8.cloned.1.call-done = bf16[512,2560]{1,0:T(8,128)(2,1)} async-done(((bf16[128,2560]{1,0:T(8,128)(2,1)}), bf16[512,2560]{1,0:T(8,128)(2,1)}) %all-gather.8.cloned.1.call-update) | async-done | bytes 2621456 | tf_op jit(solution)/shard_map/all_gather | solution.py:219
  168.0 5.5 %fusion.19 = f32[512,800]{0,1:T(8,128)S(1)} fusion(bf16[512,2560]{1,0:T(8,128)(2,1)} %all-gather.8.cloned.1.call-done, bf16[2560,800]{1,0:T(8,128)(2,1)} %all-gather.10.cloned.1.call-done), kind=kOutput, calls=%fused_computation.67 | convolution fusion | flops 2097152000 | bytes 8355840 | tf_op jit(solution)/shard_map/dot_general | solution.py:220
  173.5 45.2 %all-gather.12.cloned.1.call-done = bf16[2560,800]{1,0:T(8,128)(2,1)} async-done(((bf16[320,800]{1,0:T(8,128)(2,1)}), bf16[2560,800]{1,0:T(8,128)(2,1)}) %all-gather.12.cloned.1.call-update) | async-done | bytes 4096016 | tf_op jit(solution)/shard_map/all_gather | solution.py:227
  218.7 51.0 %all-gather.14.cloned.1.call-done = bf16[800,2560]{0,1:T(8,128)(2,1)} async-done(((bf16[800,320]{0,1:T(8,128)(2,1)}), bf16[800,2560]{0,1:T(8,128)(2,1)}) %all-gather.14.cloned.1.call-update) | async-done | bytes 4096016 | tf_op jit(solution)/shard_map/all_gather | solution.py:233
  269.7 11.2 %convolution_convert_fusion = bf16[512,2560]{1,0:T(8,128)(2,1)} fusion(bf16[800,2560]{0,1:T(8,128)(2,1)} %all-gather.14.cloned.1.call-done, f32[512,800]{0,1:T(8,128)S(1)} %fusion.19, bf16[512,2560]{1,0:T(8,128)(2,1)} %all-gather.8.cloned.1.call-done, bf16[2560,800]{1,0:T(8,128)(2,1)} %all-gather.12.cloned.1.call-done), kind=kOutput, calls=%fused_computation | convolution fusion | flops 4198072320 | bytes 15073280 | tf_op jit(solution)/shard_map/dot_general | solution.py:231
  280.9 0.9 copy-done.13
  281.9 0.6 pad_maximum_fusion.3
  282.5 38.4 %reduce-scatter.2.cloned.1.call-done = bf16[128,2560]{1,0:T(8,128)(2,1)} async-done(((bf16[512,2560]{1,0:T(8,128)(2,1)}), bf16[128,2560]{1,0:T(8,128)(2,1)}) %reduce-scatter.2.cloned.1.call-update) | async-done | bytes 655376 | tf_op jit(solution)/shard_map/reduce_scatter | solution.py:236
  320.9 2.3 fusion.8
  (85 shorter events, 2.3 us)
Async XLA Ops:
  7.2 21.5 %copy-start = (bf16[768,1920]{1,0:T(8,128)(2,1)S(1)}, bf16[768,1920]{1,0:T(8,128)(2,1)}, u32[]{:S(2)}) copy-start(bf16[768,1920]{1,0:T(8,128)(2,1)} %param.23) | copy-start | bytes 8847364
  7.2 79.1 %all-gather.6.cloned.1.call-start = ((), (), s32[]{:S(2)}) async-start(), calls=%async_computation.1 | async-start | bytes 3538944 | tf_op jit(solution)/shard_map/all_gather | solution.py:177
  9.3 119.3 %all-gather.10.cloned.1.call-start = ((), (), s32[]{:S(2)}) async-start(), calls=%async_computation.3 | async-start | bytes 5160960 | tf_op jit(solution)/shard_map/all_gather | solution.py:222
  10.0 158.0 %all-gather.8.cloned.1.call-start = ((), (), s32[]{:S(2)}) async-start(), calls=%async_computation.2 | async-start | bytes 3276800 | tf_op jit(solution)/shard_map/all_gather | solution.py:219
  20.2 5.4 %copy-start.5 = (bf16[128,2560]{1,0:T(8,128)(2,1)S(1)}, bf16[128,2560]{1,0:T(8,128)(2,1)}, u32[]{:S(2)}) copy-start(bf16[128,2560]{1,0:T(8,128)(2,1)} %param.19) | copy-start | bytes 1966084
  25.7 3.0 copy-start.18
  29.3 3.9 %copy-start.15 = (bf16[256,1280]{1,0:T(8,128)(2,1)S(1)}, bf16[256,1280]{1,0:T(8,128)(2,1)}, u32[]{:S(2)}) copy-start(bf16[256,1280]{1,0:T(8,128)(2,1)} %param.26) | copy-start | bytes 1966084
  29.6 4.7 %copy-start.11 = (bf16[128,1920]{0,1:T(8,128)(2,1)}, bf16[128,1920]{0,1:T(8,128)(2,1)S(1)}, u32[]{:S(2)}) copy-start(bf16[128,1920]{0,1:T(8,128)(2,1)S(1)} %copy.37) | copy-start | bytes 1474564
  34.4 1.9 copy-start.21
  34.4 1.9 copy-start.12
  36.2 39.3 %copy-start.20 = (s32[128]{0:T(128)S(1)}, s32[128]{0:T(128)}, u32[]{:S(2)}) copy-start(s32[128]{0:T(128)} %iota_add_fusion) | copy-start | bytes 1540
  53.8 24.2 %copy-start.17 = (bf16[2560]{0:T(1024)(128)(2,1)S(1)}, bf16[2560]{0:T(1024)(128)(2,1)}, u32[]{:S(2)}) copy-start(bf16[2560]{0:T(1024)(128)(2,1)} %param.29) | copy-start | bytes 15364
  78.0 1.9 copy-start.16
  78.0 2.0 copy-start.9
  78.0 2.0 copy-start.19
  78.0 2.2 copy-start.14
  79.9 1.1 copy-start.8
  86.3 2.4 copy-start.7
  88.7 3.6 %copy-start.2 = (bf16[1024,512]{1,0:T(8,128)(2,1)S(1)}, bf16[1024,512]{1,0:T(8,128)(2,1)}, u32[]{:S(2)}) copy-start(bf16[1024,512]{1,0:T(8,128)(2,1)} %get-tuple-element.6.span_ref) | copy-start | bytes 3145732
  88.7 3.6 %copy-start.3 = (bf16[1024,512]{1,0:T(8,128)(2,1)S(1)}, bf16[1024,512]{1,0:T(8,128)(2,1)}, u32[]{:S(2)}) copy-start(bf16[1024,512]{1,0:T(8,128)(2,1)} %get-tuple-element.7.prompt_ref) | copy-start | bytes 3145732
  92.3 32.0 %slice-start = ((s8[6553600]{0:T(1024)(128)(4,1)}), s8[4194304]{0:T(1024)(128)(4,1)S(1)}, s32[]{:S(2)}) async-start(s8[6553600]{0:T(1024)(128)(4,1)} %bitcast.40), calls=%async_computation.7 | async-start | bytes 8388608
  92.3 31.4 %copy-start.10 = (bf16[256,1280]{0,1:T(8,128)(2,1)S(1)}, bf16[256,1280]{0,1:T(8,128)(2,1)}, u32[]{:S(2)}) copy-start(bf16[256,1280]{0,1:T(8,128)(2,1)} %copy.43) | copy-start | bytes 1966084
  92.3 31.9 %slice-start.1 = ((s8[6553600]{0:T(1024)(128)(4,1)}), s8[2359296]{0:T(1024)(128)(4,1)S(1)}, s32[]{:S(2)}) async-start(s8[6553600]{0:T(1024)(128)(4,1)} %bitcast.40), calls=%async_computation.8 | async-start | bytes 4718592
  123.6 1.1 copy-start.6
  125.8 47.7 %copy-start.4 = (bf16[128,2560]{1,0:T(8,128)(2,1)}, bf16[128,2560]{1,0:T(8,128)(2,1)S(1)}, u32[]{:S(2)}) copy-start(bf16[128,2560]{1,0:T(8,128)(2,1)S(1)} %fusion.1) | copy-start | bytes 1966084
  127.1 91.6 %all-gather.12.cloned.1.call-start = ((), (), s32[]{:S(2)}) async-start(), calls=%async_computation.4 | async-start | bytes 5160960 | tf_op jit(solution)/shard_map/all_gather | solution.py:227
  127.7 142.0 %all-gather.14.cloned.1.call-start = ((), (), s32[]{:S(2)}) async-start(), calls=%async_computation.5 | async-start | bytes 5160960 | tf_op jit(solution)/shard_map/all_gather | solution.py:233
  128.3 192.7 %reduce-scatter.2.cloned.1.call-start = ((), (), s32[]{:S(2)}) async-start(), calls=%async_computation.6 | async-start | bytes 3276800 | tf_op jit(solution)/shard_map/reduce_scatter | solution.py:236
  280.9 0.9 copy-start.13
  280.9 42.3 %copy-start.1 = (bf16[768,1920]{1,0:T(8,128)(2,1)S(1)}, bf16[768,1920]{1,0:T(8,128)(2,1)}, u32[]{:S(2)}) copy-start(bf16[768,1920]{1,0:T(8,128)(2,1)} %param.23) | copy-start | bytes 8847364
Sparse Core Ops, SparseCore 0:
  9.7 42.1 all-gather.5
  53.5 53.2 all-gather.9
  127.2 40.7 all-gather.7
  169.5 49.1 all-gather.11
  220.2 49.4 all-gather.13
  281.0 39.8 reduce-scatter.1

commit v2 on v1

--- a/solution.py
+++ b/solution.py
@@ -89,6 +89,94 @@
         ),
         compiler_params=pltpu.CompilerParams(vmem_limit_bytes=48 * 2**20),
     )(queries, prompt_keys, cache_keys, span_keys)
+
+
+def feed_forward_kernel(
+    post_ref, residual_ref, gate_ref, up_ref, down_ref, out_ref,
+    rows_in, part_out, part_in, own, row_send, row_recv, part_send, part_recv,
+):
+    groups = rows_in.shape[0] + 1
+    me = lax.axis_index("grp")
+
+    def device(step):
+        return {"grp": lax.rem(me + step + groups, groups)}
+
+    def row_copy(step):
+        return pltpu.make_async_remote_copy(
+            src_ref=post_ref,
+            dst_ref=rows_in.at[step - 1],
+            send_sem=row_send.at[step - 1],
+            recv_sem=row_recv.at[step - 1],
+            device_id=device(step),
+            device_id_type=pl.DeviceIdType.MESH,
+        )
+
+    def part_copy(step):
+        return pltpu.make_async_remote_copy(
+            src_ref=part_out.at[step - 1],
+            dst_ref=part_in.at[step - 1],
+            send_sem=part_send.at[step - 1],
+            recv_sem=part_recv.at[step - 1],
+            device_id=device(-step),
+            device_id_type=pl.DeviceIdType.MESH,
+        )
+
+    def layer(rows):
+        gate = jnp.dot(rows, gate_ref[...], preferred_element_type=jnp.float32)
+        up = jnp.dot(rows, up_ref[...], preferred_element_type=jnp.float32)
+        hidden = (gate / (1.0 + jnp.exp(-gate)) * up).astype(jnp.bfloat16)
+        return jnp.dot(hidden, down_ref[...], preferred_element_type=jnp.float32)
+
+    barrier = pltpu.get_barrier_semaphore()
+    for step in range(1, groups):
+        pl.semaphore_signal(
+            barrier, inc=1, device_id=device(step), device_id_type=pl.DeviceIdType.MESH
+        )
+    pl.semaphore_wait(barrier, groups - 1)
+    for step in range(1, groups):
+        row_copy(step).start()
+    own[...] = layer(post_ref[...]) + residual_ref[...].astype(jnp.float32)
+
+    @pl.loop(1, groups)
+    def _(step):
+        row_copy(step).wait_recv()
+        part_out[step - 1] = layer(rows_in[step - 1]).astype(jnp.bfloat16)
+        part_copy(step).start()
+
+    @pl.loop(1, groups)
+    def _(step):
+        part_copy(step).wait_recv()
+        own[...] += part_in[step - 1].astype(jnp.float32)
+        part_copy(step).wait_send()
+        row_copy(step).wait_send()
+
+    out_ref[...] = own[...].astype(jnp.bfloat16)
+
+
+def feed_forward(post_norm, residual, gate, up, down):
+    groups = lax.axis_size("grp")
+    slots = (groups - 1,) + post_norm.shape
+    return pl.pallas_call(
+        feed_forward_kernel,
+        out_shape=jax.ShapeDtypeStruct(post_norm.shape, jnp.bfloat16),
+        in_specs=[pl.BlockSpec(memory_space=pltpu.VMEM)] * 5,
+        out_specs=pl.BlockSpec(memory_space=pltpu.VMEM),
+        scratch_shapes=[
+            pltpu.VMEM(slots, jnp.bfloat16),
+            pltpu.VMEM(slots, jnp.bfloat16),
+            pltpu.VMEM(slots, jnp.bfloat16),
+            pltpu.VMEM(post_norm.shape, jnp.float32),
+        ]
+        + [pltpu.SemaphoreType.DMA((groups - 1,))] * 4,
+        cost_estimate=pl.CostEstimate(
+            flops=6 * groups * post_norm.shape[0] * gate.size,
+            bytes_accessed=2**24,
+            transcendentals=0,
+        ),
+        compiler_params=pltpu.CompilerParams(
+            collective_id=1, has_side_effects=True, vmem_limit_bytes=48 * 2**20
+        ),
+    )(post_norm, residual, gate, up, down)
 
 
 def widened(key_rows, live, hidden_at):
@@ -216,27 +304,13 @@
         (tokens.astype(jnp.float32) + attended).astype(jnp.bfloat16)
     )
     post_norm = norm_rows(residual.astype(jnp.float32), post_gain).astype(jnp.bfloat16)
-    rows_all = lax.all_gather(post_norm, "grp", axis=0, tiled=True)
-    gate_values = jnp.dot(
-        rows_all,
+    layer_out = feed_forward(
+        post_norm,
+        residual,
         lax.all_gather(gate_weight, "tok", axis=0, tiled=True),
-        preferred_element_type=jnp.float32,
-    )
-    up_values = jnp.dot(
-        rows_all,
         lax.all_gather(up_weight, "tok", axis=0, tiled=True),
-        preferred_element_type=jnp.float32,
-    )
-    hidden = (jax.nn.silu(gate_values) * up_values).astype(jnp.bfloat16)
-    partial_out = jnp.dot(
-        hidden,
         lax.all_gather(down_weight, "tok", axis=1, tiled=True),
-        preferred_element_type=jnp.float32,
-    )
-    down_values = lax.psum_scatter(
-        partial_out.astype(jnp.bfloat16), "grp", scatter_dimension=0, tiled=True
-    ).astype(jnp.float32)
-    layer_out = (residual.astype(jnp.float32) + down_values).astype(jnp.bfloat16)
+    )
     return (layer_out, new_latents)
 
 

time: 332 us -> 292 us (0.88)
  waiting for transfers between devices: 176 us -> 77.9 us
  Pallas kernels: 31.3 us -> 100 us
  matrix products: 26.6 us -> 9.56 us
  local copies, waits for them, and re-layouts: 15.5 us -> 26.1 us
  other arithmetic: 25.6 us -> 21 us
    pallas_call x0 -> x1, Pallas kernels: none -> 68.8 us  [feed_forward(): pl.pallas_call(feed_forward_kernel, out_shape=jax.ShapeDtypeStruct(post_n...]
    all_gather x1, waiting for transfers between devices: 51 us -> 0.01 us  [body(): lax.all_gather(down_weight, 'tok', axis=1, tiled=True)]
    all_gather x1 -> x0, waiting for transfers between devices: 39.5 us -> none  [body(): rows_all = lax.all_gather(post_norm, 'grp', axis=0, tiled=True)]
    reduce_scatter x1 -> x0, waiting for transfers between devices: 38.4 us -> none  [body(): lax.psum_scatter(partial_out.astype(jnp.bfloat16), 'grp', scatter_dimensi...]
    all_gather x1, waiting for transfers between devices: 0.02 us -> 25 us  [body(): lax.all_gather(gate_weight, 'tok', axis=0, tiled=True)]
    dot_general x2 -> x0, matrix products: 16.7 us -> none  [the longest x1 11.2 us: body(): jnp.dot(hidden, lax.all_gather(down_weight, 'tok', axis=1, tiled=True), p...]
    all_gather x0 -> x1, local copies, waits for them, and re-layouts: none -> 7.17 us  [body(): lax.all_gather(down_weight, 'tok', axis=1, tiled=True)]
    all_gather x1, waiting for transfers between devices: 45.2 us -> 51 us  [body(): lax.all_gather(up_weight, 'tok', axis=0, tiled=True)]
  transfers between devices with their start and end apart: 6 -> 4, of which waited for: 4 -> 2; matrix products, arithmetic and copies ran while one was open for 15% -> 16% of each run, Pallas kernels for 9% -> 11%
where the time goes in v2:
time: 292 us; the launch traced here: 288 us
  Pallas kernels  100 us (34%)
  waiting for transfers between devices  77.9 us (27%)
  blocking collectives  36.1 us (12%)
  local copies, waits for them, and re-layouts  26.1 us (9%)
  other arithmetic  21 us (7%)
  between operations  17.3 us (6%)
  matrix products  9.56 us (3%)
    pallas_call x1, Pallas kernels, feed_forward(): pl.pallas_call(feed_forward_kernel, out_shape=jax.ShapeDtypeStruct(post_n...  68.8 us
    all_gather x1, waiting for transfers between devices, body(): lax.all_gather(up_weight, 'tok', axis=0, tiled=True)  51 us
    pallas_call x1, Pallas kernels, flash(): pl.pallas_call(functools.partial(flash_kernel, 512, 512), out_shape=jax.S...  31.2 us
    all_gather x1, waiting for transfers between devices, body(): lax.all_gather(gate_weight, 'tok', axis=0, tiled=True)  25 us
    all_gather x1, blocking collectives, body(): span_all = lax.all_gather(new_latents, 'tok', axis=0)  18.1 us
    all_gather x1, blocking collectives, body(): prompt_all = lax.all_gather(group_prompts, 'tok', axis=1, tiled=True)  18 us
    unnamed x61, local copies, waits for them, and re-layouts  13 us
    all_gather x1, local copies, waits for them, and re-layouts, body(): lax.all_gather(down_weight, 'tok', axis=1, tiled=True)  7.17 us
  transfers between devices with their start and end apart: 4, of which 2 were waited for; matrix products, arithmetic and copies ran while one was open for 16% of the time, Pallas kernels for 11%

profile of v2, /device:TPU:8, one launch (start us, length us, event | category | flops | bytes accessed | tf_op | source)
XLA Modules:
  0.0 288.2 jit_solution(1208596321925888200)
XLA Ops:
  7.3 2.0 copy.43
  9.4 0.7 all-gather.11.cloned.1.call-update
  10.1 0.7 all-gather.7.cloned.1.call-update
  10.9 0.5 all-gather.9.cloned.1.call-update
  11.4 0.6 fusion.16
  12.0 0.6 dynamic_slice.19
  14.6 0.6 dynamic_slice.20
  15.2 0.6 iota_compare_fusion.5
  15.8 1.4 select_convert_fusion.2
  17.2 1.3 fusion.5
  18.6 2.5 fusion.12
  21.2 0.5 copy-done.14
  21.7 0.7 multiply_convert_fusion.2
  22.4 0.6 dynamic_slice.21
  24.2 3.1 %multiply_reduce_fusion = (f32[128]{0:T(128)S(1)}, f32[128,768]{1,0:T(8,128)S(1)}) fusion(bf16[2560,768]{1,0:T(8,128)(2,1)} %param.21, bf16[128,2560]{1,0:T(8,128)(2,1)} %param.19, f32[2560]{0:T(1024)S(1)} %convert_element_type.93, f32[128]{0:T(128)S(1)} %add_rsqrt_fusion.3), kind=kOutput, calls=%fused_computation.29 | convolution fusion | flops 504823680 | bytes 4992000 | tf_op jit(solution)/shard_map/dot_general | solution.py:225
  27.4 0.6 convolution_convert_fusion
  28.3 0.9 subtract_convert_fusion
  29.4 1.5 copy.41
  30.9 1.1 copy.40
  32.0 1.7 fusion.8
  33.7 18.1 %all_gather.21 = bf16[8,128,288]{1,2,0:T(8,128)(2,1)S(1)} all-gather(bf16[1,128,288]{1,2,0:T(8,128)(2,1)S(1)} %pad_maximum_fusion.2), channel_id=1, replica_groups=mesh['grp'=4,'tok'=8] {'tok'}, dimensions={0}, use_global_device_ids=true | all-gather | bytes 663552 | tf_op jit(solution)/shard_map/all_gather | solution.py:267
  51.8 1.2 copy.44
  53.0 0.9 constant_dynamic-slice_fusion
  54.0 18.0 %all_gather.19 = bf16[1,1024,288]{2,1,0:T(8,128)(2,1)} all-gather(bf16[1,128,288]{2,1,0:T(8,128)(2,1)S(1)} %copy.47), channel_id=1, replica_groups=mesh['grp'=4,'tok'=8] {'tok'}, dimensions={1}, use_global_device_ids=true | all-gather | bytes 663552 | tf_op jit(solution)/shard_map/all_gather | solution.py:266
  72.4 2.2 copy.45
  74.5 0.6 pad_maximum_fusion.3
  75.2 1.8 fusion
  77.4 0.8 copy-done.10
  78.2 1.8 pad_maximum_fusion.1
  80.0 0.6 iota_compare_fusion.4
  80.7 0.8 pad_maximum_fusion.q_ref
  81.5 1.8 select_convert_fusion
  83.3 2.3 bitcast_select_fusion
  85.7 3.5 %maximum_maximum_fusion.cache_ref = bf16[4096,512]{1,0:T(8,128)(2,1)} fusion(bf16[4096,1]{1,0:T(8,128)(2,1)S(1)} %copy-done.9, bf16[4096,288]{1,0:T(8,128)(2,1)S(1)} %bitcast_select_fusion, bf16[512]{0:T(512)(128)(2,1)S(1)} %pad.17.clone, bf16[512]{0:T(512)(128)(2,1)S(1)} %pad.16.clone), kind=kLoop, calls=%fused_computation | loop fusion | flops 16777216 | bytes 6563840 | tf_op jit(solution)/shard_map/concatenate | solution.py:186
  89.2 31.2 %shard_map.194 = bf16[2560,256]{1,0:T(8,128)(2,1)S(1)} custom-call(bf16[2560,512]{1,0:T(8,128)(2,1)S(1)} %pad_maximum_fusion.q_ref, bf16[1024,512]{1,0:T(8,128)(2,1)S(1)} %copy-done.6, bf16[4096,512]{1,0:T(8,128)(2,1)} %maximum_maximum_fusion.cache_ref, bf16[1024,512]{1,0:T(8,128)(2,1)S(1)} %copy-done.5), custom_call_target="tpu_custom_call" | custom-call | flops 24159191040 | bytes 16777216 | tf_op jit(solution)/shard_map/pallas_call | solution.py:82
  120.5 0.6 convolution_convert_fusion.1
  121.1 0.5 copy-done.8
  121.6 1.0 fusion.1.residual_ref
  122.8 0.6 copy-done.2
  123.4 1.1 fusion.4.post_ref
  124.5 7.2 %copy.46.down_ref = bf16[800,2560]{1,0:T(8,128)(2,1)} copy(bf16[800,2560]{0,1:T(8,128)(2,1)} %all-gather.11.cloned.1.call-done) | data formatting | bytes 8192000 | tf_op jit(solution)/shard_map/all_gather | solution.py:312
  131.7 25.0 %all-gather.7.cloned.1.call-done.gate_ref = bf16[2560,800]{1,0:T(8,128)(2,1)} async-done(((bf16[320,800]{1,0:T(8,128)(2,1)}), bf16[2560,800]{1,0:T(8,128)(2,1)}) %all-gather.7.cloned.1.call-update) | async-done | bytes 4096016 | tf_op jit(solution)/shard_map/all_gather | solution.py:310
  156.7 51.0 %all-gather.9.cloned.1.call-done.up_ref = bf16[2560,800]{1,0:T(8,128)(2,1)} async-done(((bf16[320,800]{1,0:T(8,128)(2,1)}), bf16[2560,800]{1,0:T(8,128)(2,1)}) %all-gather.9.cloned.1.call-update) | async-done | bytes 4096016 | tf_op jit(solution)/shard_map/all_gather | solution.py:311
  207.7 1.1 copy-done.3
  208.8 2.2 copy-done.4
  210.9 1.1 copy-done.7
  212.0 68.8 %shard_map.195 = bf16[128,2560]{1,0:T(8,128)(2,1)S(1)} custom-call(bf16[128,2560]{1,0:T(8,128)(2,1)S(1)} %copy-done.7, bf16[128,2560]{1,0:T(8,128)(2,1)S(1)} %copy-done.3, bf16[2560,800]{1,0:T(8,128)(2,1)} %all-gather.7.cloned.1.call-done.gate_ref, bf16[2560,800]{1,0:T(8,128)(2,1)} %all-gather.9.cloned.1.call-done.up_ref, bf16[800,2560]{1,0:T(8,128)(2,1)S(1)} %copy-done.4), custom_call_target="tpu_custom_call" | custom-call | flops 6291456000 | bytes 16777216 | tf_op jit(solution)/shard_map/pallas_call | solution.py:159
  280.8 0.8 copy.49
  (87 shorter events, 2.0 us)
Async XLA Ops:
  7.2 20.2 %copy-start = (bf16[768,1920]{1,0:T(8,128)(2,1)S(1)}, bf16[768,1920]{1,0:T(8,128)(2,1)}, u32[]{:S(2)}) copy-start(bf16[768,1920]{1,0:T(8,128)(2,1)} %param.23) | copy-start | bytes 8847364
  7.2 4.9 %copy-start.22 = (s32[4]{0:T(128)S(1)}, s32[4]{0:T(128)}, u32[]{:S(2)}) copy-start(s32[4]{0:T(128)} %param.37) | copy-start | bytes 52
  7.2 7.4 %copy-start.23 = (s32[8]{0:T(128)S(1)}, s32[8]{0:T(128)}, u32[]{:S(2)}) copy-start(s32[8]{0:T(128)} %param.36) | copy-start | bytes 100
  7.2 10.0 %copy-start.19 = (bf16[2560]{0:T(1024)(128)(2,1)S(1)}, bf16[2560]{0:T(1024)(128)(2,1)}, u32[]{:S(2)}) copy-start(bf16[2560]{0:T(1024)(128)(2,1)} %param.20) | copy-start | bytes 15364
  7.2 76.1 %all-gather.5.cloned.1.call-start = ((), (), s32[]{:S(2)}) async-start(), calls=%async_computation | async-start | bytes 3538944 | tf_op jit(solution)/shard_map/all_gather | solution.py:265
  9.3 115.2 %all-gather.11.cloned.1.call-start = ((), (), s32[]{:S(2)}) async-start(), calls=%async_computation.3 | async-start | bytes 5160960 | tf_op jit(solution)/shard_map/all_gather | solution.py:312
  10.1 146.6 %all-gather.7.cloned.1.call-start = ((), (), s32[]{:S(2)}) async-start(), calls=%async_computation.1 | async-start | bytes 5160960 | tf_op jit(solution)/shard_map/all_gather | solution.py:310
  10.8 10.3 %copy-start.24 = (bf16[256]{0:T(256)(128)(2,1)S(1)}, bf16[256]{0:T(256)(128)(2,1)}, u32[]{:S(2)}) copy-start(bf16[256]{0:T(256)(128)(2,1)} %param.25) | copy-start | bytes 1540
  10.8 196.9 %all-gather.9.cloned.1.call-start = ((), (), s32[]{:S(2)}) async-start(), calls=%async_computation.2 | async-start | bytes 5160960 | tf_op jit(solution)/shard_map/all_gather | solution.py:311
  11.4 11.0 %copy-start.25 = (s32[4]{0:T(128)S(1)}, s32[4]{0:T(128)}, u32[]{:S(2)}) copy-start(s32[4]{0:T(128)} %param.35) | copy-start | bytes 52
  21.0 0.7 copy-start.14
  24.2 3.2 %copy-start.21 = (bf16[768]{0:T(1024)(128)(2,1)S(1)}, bf16[768]{0:T(1024)(128)(2,1)}, u32[]{:S(2)}) copy-start(bf16[768]{0:T(1024)(128)(2,1)} %param.22) | copy-start | bytes 4612
  28.0 2.9 copy-start.16
  28.3 3.7 %copy-start.13 = (bf16[128,1920]{0,1:T(8,128)(2,1)}, bf16[128,1920]{0,1:T(8,128)(2,1)S(1)}, u32[]{:S(2)}) copy-start(bf16[128,1920]{0,1:T(8,128)(2,1)S(1)} %copy.39) | copy-start | bytes 1474564
  51.8 22.7 %copy-start.20 = (bf16[2560]{0:T(1024)(128)(2,1)S(1)}, bf16[2560]{0:T(1024)(128)(2,1)}, u32[]{:S(2)}) copy-start(bf16[2560]{0:T(1024)(128)(2,1)} %param.29) | copy-start | bytes 15364
  51.8 22.7 %copy-start.17 = (bf16[128,256]{0,1:T(8,128)(2,1)S(1)}, bf16[128,256]{0,1:T(8,128)(2,1)}, u32[]{:S(2)}) copy-start(bf16[128,256]{0,1:T(8,128)(2,1)} %multiply_convert_fusion.2) | copy-start | bytes 196612
  75.2 1.9 copy-start.18
  75.2 2.0 copy-start.11
  75.2 2.2 copy-start.15
  77.0 1.1 copy-start.10
  83.3 2.4 copy-start.9
  85.7 3.5 %copy-start.5 = (bf16[1024,512]{1,0:T(8,128)(2,1)S(1)}, bf16[1024,512]{1,0:T(8,128)(2,1)}, u32[]{:S(2)}) copy-start(bf16[1024,512]{1,0:T(8,128)(2,1)} %get-tuple-element.6.span_ref) | copy-start | bytes 3145732
  85.7 3.5 %copy-start.6 = (bf16[1024,512]{1,0:T(8,128)(2,1)S(1)}, bf16[1024,512]{1,0:T(8,128)(2,1)}, u32[]{:S(2)}) copy-start(bf16[1024,512]{1,0:T(8,128)(2,1)} %get-tuple-element.7.prompt_ref) | copy-start | bytes 3145732
  89.2 31.9 %slice-start = ((s8[6553600]{0:T(1024)(128)(4,1)}), s8[4194304]{0:T(1024)(128)(4,1)S(1)}, s32[]{:S(2)}) async-start(s8[6553600]{0:T(1024)(128)(4,1)} %bitcast.35), calls=%async_computation.4 | async-start | bytes 8388608
  89.2 31.3 %copy-start.12 = (bf16[256,1280]{0,1:T(8,128)(2,1)S(1)}, bf16[256,1280]{0,1:T(8,128)(2,1)}, u32[]{:S(2)}) copy-start(bf16[256,1280]{0,1:T(8,128)(2,1)} %copy.45) | copy-start | bytes 1966084
  89.2 31.9 %slice-start.1 = ((s8[6553600]{0:T(1024)(128)(4,1)}), s8[2359296]{0:T(1024)(128)(4,1)S(1)}, s32[]{:S(2)}) async-start(s8[6553600]{0:T(1024)(128)(4,1)} %bitcast.35), calls=%async_computation.5 | async-start | bytes 4718592
  120.5 1.1 copy-start.8
  122.6 0.8 copy-start.2
  207.7 1.1 copy-start.3
  208.8 2.2 copy-start.4
  210.9 1.1 copy-start.7
  212.0 69.6 %copy-start.1 = (bf16[768,1920]{1,0:T(8,128)(2,1)S(1)}, bf16[768,1920]{1,0:T(8,128)(2,1)}, u32[]{:S(2)}) copy-start(bf16[768,1920]{1,0:T(8,128)(2,1)} %param.23) | copy-start | bytes 8847364
Sparse Core Ops, SparseCore 0:
  9.7 43.2 all-gather.4
  54.6 50.6 all-gather.10
  106.9 49.7 all-gather.6
  158.2 49.4 all-gather.8

commit v3 on v2

--- a/solution.py
+++ b/solution.py
@@ -39,7 +39,36 @@
     )
 
 
-def flash_kernel(row_block, key_block, q_ref, prompt_ref, cache_ref, span_ref, out_ref):
+def flash_kernel(
+    row_block, key_block, q_ref, prompt_ref, cache_ref, span_ref, shard_ref,
+    out_ref, whole_ref, own_sem, send_sem, recv_sem,
+):
+    devices = whole_ref.shape[0]
+    me = lax.axis_index("tok")
+
+    def shard_copy(step):
+        return pltpu.make_async_remote_copy(
+            src_ref=shard_ref,
+            dst_ref=whole_ref.at[me],
+            send_sem=send_sem.at[step - 1],
+            recv_sem=recv_sem.at[step - 1],
+            device_id={"tok": lax.rem(me + step, devices)},
+            device_id_type=pl.DeviceIdType.MESH,
+        )
+
+    own_copy = pltpu.make_async_copy(shard_ref, whole_ref.at[me], own_sem)
+    own_copy.start()
+    barrier = pltpu.get_barrier_semaphore()
+    for step in range(1, devices):
+        pl.semaphore_signal(
+            barrier,
+            inc=1,
+            device_id={"tok": lax.rem(me + step, devices)},
+            device_id_type=pl.DeviceIdType.MESH,
+        )
+    pl.semaphore_wait(barrier, devices - 1)
+    for step in range(1, devices):
+        shard_copy(step).start()
     segments = []
     for ref in (prompt_ref, cache_ref, span_ref):
         for first in range(0, ref.shape[0], key_block):
@@ -75,20 +104,39 @@
             largest, scores = new_max, following
         out_ref[rows, :] = (mixed / total).astype(jnp.bfloat16)
 
-
-def flash(queries, prompt_keys, cache_keys, span_keys):
+    own_copy.wait()
+    for step in range(1, devices):
+        shard_copy(step).wait()
+
+
+def flash(queries, prompt_keys, cache_keys, span_keys, shard):
+    devices = lax.axis_size("tok")
     rows = queries.shape[0]
     count = prompt_keys.shape[0] + cache_keys.shape[0] + span_keys.shape[0]
     return pl.pallas_call(
         functools.partial(flash_kernel, 512, 512),
-        out_shape=jax.ShapeDtypeStruct((rows, KVR), jnp.bfloat16),
-        in_specs=[pl.BlockSpec(memory_space=pltpu.VMEM)] * 4,
-        out_specs=pl.BlockSpec(memory_space=pltpu.VMEM),
+        out_shape=(
+            jax.ShapeDtypeStruct((rows, KVR), jnp.bfloat16),
+            jax.ShapeDtypeStruct((devices,) + shard.shape, shard.dtype),
+        ),
+        in_specs=[pl.BlockSpec(memory_space=pltpu.VMEM)] * 4
+        + [pl.BlockSpec(memory_space=pl.ANY)],
+        out_specs=(
+            pl.BlockSpec(memory_space=pltpu.VMEM),
+            pl.BlockSpec(memory_space=pl.ANY),
+        ),
+        scratch_shapes=[
+            pltpu.SemaphoreType.DMA,
+            pltpu.SemaphoreType.DMA((devices - 1,)),
+            pltpu.SemaphoreType.DMA((devices - 1,)),
+        ],
         cost_estimate=pl.CostEstimate(
             flops=2 * rows * count * 768, bytes_accessed=2**24, transcendentals=rows * count
         ),
-        compiler_params=pltpu.CompilerParams(vmem_limit_bytes=48 * 2**20),
-    )(queries, prompt_keys, cache_keys, span_keys)
+        compiler_params=pltpu.CompilerParams(
+            collective_id=2, has_side_effects=True, vmem_limit_bytes=48 * 2**20
+        ),
+    )(queries, prompt_keys, cache_keys, span_keys, shard)
 
 
 def feed_forward_kernel(
@@ -277,7 +325,7 @@
     hidden = jnp.where(span_place[:, None] <= within[None, :], 0.0, -1e30).astype(jnp.bfloat16)
     prompt_live_rows = jnp.arange(prompt_rows.shape[0], dtype=jnp.int32) < prompt_live
     cache_live_rows = jnp.arange(cache_rows.shape[0], dtype=jnp.int32) < cache_live
-    latent_out = flash(
+    latent_out, up_all = flash(
         query_rows,
         widened(
             prompt_rows,
@@ -288,7 +336,9 @@
             cache_rows, cache_live_rows, jnp.zeros((cache_rows.shape[0], tok_dev), jnp.bfloat16)
         ),
         widened(span_rows, span_place >= 0, hidden),
-    ).reshape(HEADS, tok_dev, KVR)
+        up_weight,
+    )
+    latent_out = latent_out.reshape(HEADS, tok_dev, KVR)
     heads_out = (
         jnp.einsum(
             "htk,khv->thv",
@@ -308,7 +358,7 @@
         post_norm,
         residual,
         lax.all_gather(gate_weight, "tok", axis=0, tiled=True),
-        lax.all_gather(up_weight, "tok", axis=0, tiled=True),
+        up_all.reshape(-1, up_weight.shape[1]),
         lax.all_gather(down_weight, "tok", axis=1, tiled=True),
     )
     return (layer_out, new_latents)

time: 292 us -> 331 us (1.13)
  Pallas kernels: 100 us -> 218 us
  waiting for transfers between devices: 77.9 us -> 1.4 us
    pallas_call x1, Pallas kernels: 31.2 us -> 149 us  [flash(): pl.pallas_call(functools.partial(flash_kernel, 512, 512), out_shape=(jax....]
    all_gather x1 -> x0, waiting for transfers between devices: 51 us -> none  [body(): lax.all_gather(up_weight, 'tok', axis=0, tiled=True)]
    all_gather x1, waiting for transfers between devices: 25 us -> 0.01 us  [body(): lax.all_gather(gate_weight, 'tok', axis=0, tiled=True)]
    unnamed x61 -> x59, local copies, waits for them, and re-layouts: 13 us -> 13 us
  transfers between devices with their start and end apart: 4 -> 3, of which waited for: 2 -> 0; matrix products, arithmetic and copies ran while one was open for 16% -> 14% of each run, Pallas kernels for 11% -> 45%
where the time goes in v3:
time: 331 us; the launch traced here: 330 us
  Pallas kernels  218 us (66%)
  blocking collectives  36.2 us (11%)
  local copies, waits for them, and re-layouts  26.1 us (8%)
  other arithmetic  21.4 us (6%)
  between operations  17.4 us (5%)
  matrix products  9.42 us (3%)
    pallas_call x1, Pallas kernels, flash(): pl.pallas_call(functools.partial(flash_kernel, 512, 512), out_shape=(jax....  149 us
    pallas_call x1, Pallas kernels, feed_forward(): pl.pallas_call(feed_forward_kernel, out_shape=jax.ShapeDtypeStruct(post_n...  69.7 us
    all_gather x1, blocking collectives, body(): prompt_all = lax.all_gather(group_prompts, 'tok', axis=1, tiled=True)  18.5 us
    all_gather x1, blocking collectives, body(): span_all = lax.all_gather(new_latents, 'tok', axis=0)  17.7 us
    unnamed x59, local copies, waits for them, and re-layouts  13 us
    all_gather x1, local copies, waits for them, and re-layouts, body(): lax.all_gather(down_weight, 'tok', axis=1, tiled=True)  7.11 us
  transfers between devices with their start and end apart: 3, of which 0 were waited for; matrix products, arithmetic and copies ran while one was open for 14% of the time, Pallas kernels for 45%

profile of v3, /device:TPU:8, one launch (start us, length us, event | category | flops | bytes accessed | tf_op | source)
XLA Modules:
  0.0 330.3 jit_solution(17559338442908503417)
XLA Ops:
  7.3 2.0 copy.43
  9.4 0.7 all-gather.8.cloned.1.call-update
  10.1 0.7 all-gather.6.cloned.1.call-update
  10.9 0.6 fusion.16
  11.5 0.6 dynamic_slice.19
  14.0 0.7 dynamic_slice.20
  14.7 0.7 iota_compare_fusion.5
  15.4 1.5 select_convert_fusion.2
  16.8 1.3 fusion.5
  18.2 2.3 fusion.12
  20.6 0.5 copy-done.13
  21.1 0.7 multiply_convert_fusion.2
  21.9 0.6 dynamic_slice.21
  23.7 3.2 multiply_reduce_fusion
  27.0 0.6 convolution_convert_fusion
  27.6 0.3 copy.39
  27.9 0.9 subtract_convert_fusion
  28.9 1.5 copy.41
  30.5 1.1 copy.40
  31.5 1.7 fusion.8
  33.3 17.7 %all_gather.18 = bf16[8,128,288]{1,2,0:T(8,128)(2,1)S(1)} all-gather(bf16[1,128,288]{1,2,0:T(8,128)(2,1)S(1)} %pad_maximum_fusion.2), channel_id=1, replica_groups=mesh['grp'=4,'tok'=8] {'tok'}, dimensions={0}, use_global_device_ids=true | all-gather | bytes 663552 | tf_op jit(solution)/shard_map/all_gather | solution.py:315
  51.0 1.1 copy.44
  52.1 0.9 constant_dynamic-slice_fusion
  53.2 18.5 %all_gather.16 = bf16[1,1024,288]{2,1,0:T(8,128)(2,1)} all-gather(bf16[1,128,288]{2,1,0:T(8,128)(2,1)S(1)} %copy.47), channel_id=1, replica_groups=mesh['grp'=4,'tok'=8] {'tok'}, dimensions={1}, use_global_device_ids=true | all-gather | bytes 663552 | tf_op jit(solution)/shard_map/all_gather | solution.py:314
  72.0 2.2 copy.45
  74.1 0.6 pad_maximum_fusion.3
  74.8 1.8 fusion
  76.8 0.2 bitcast_select_fusion.1
  77.0 0.8 copy-done.9
  77.8 0.7 pad_maximum_fusion.1
  78.4 0.6 iota_compare_fusion.4
  79.1 2.2 pad_maximum_fusion.q_ref
  81.3 1.9 select_convert_fusion
  83.2 2.3 bitcast_select_fusion
  85.6 3.5 %maximum_maximum_fusion.cache_ref = bf16[4096,512]{1,0:T(8,128)(2,1)} fusion(bf16[4096,1]{1,0:T(8,128)(2,1)S(1)} %copy-done.8, bf16[4096,288]{1,0:T(8,128)(2,1)S(1)} %bitcast_select_fusion, bf16[512]{0:T(512)(128)(2,1)S(1)} %pad.17.clone, bf16[512]{0:T(512)(128)(2,1)S(1)} %pad.16.clone), kind=kLoop, calls=%fused_computation | loop fusion | flops 16777216 | bytes 6563840 | tf_op jit(solution)/shard_map/concatenate | solution.py:234
  89.1 148.6 %shard_map.194 = (bf16[2560,256]{1,0:T(8,128)(2,1)S(1)}, bf16[8,320,800]{2,1,0:T(8,128)(2,1)}) custom-call(bf16[2560,512]{1,0:T(8,128)(2,1)} %pad_maximum_fusion.q_ref, bf16[1024,512]{1,0:T(8,128)(2,1)S(1)} %get-tuple-element.11.prompt_ref, bf16[4096,512]{1,0:T(8,128)(2,1)} %maximum_maximum_fusion.cache_ref, ...), custom_call_target="tpu_custom_call" | custom-call | flops 24159191040 | bytes 16777216 | tf_op jit(solution)/shard_map/pallas_call | solution.py:116
  237.7 0.6 convolution_convert_fusion.1
  238.3 0.5 copy-done.7
  238.7 1.0 fusion.1.residual_ref
  239.8 0.2 fusion.2
  240.0 0.6 copy-done.2
  240.6 1.1 fusion.4.post_ref
  241.7 7.1 %copy.46.down_ref = bf16[800,2560]{1,0:T(8,128)(2,1)} copy(bf16[800,2560]{0,1:T(8,128)(2,1)} %all-gather.8.cloned.1.call-done) | data formatting | bytes 8192000 | tf_op jit(solution)/shard_map/all_gather | solution.py:362
  248.8 1.1 copy-done.3
  249.9 2.2 copy-done.4
  252.1 1.1 copy-done.5
  253.2 69.7 %shard_map.195 = bf16[128,2560]{1,0:T(8,128)(2,1)S(1)} custom-call(bf16[128,2560]{1,0:T(8,128)(2,1)S(1)} %copy-done.5, bf16[128,2560]{1,0:T(8,128)(2,1)S(1)} %copy-done.3, bf16[2560,800]{1,0:T(8,128)(2,1)} %all-gather.6.cloned.1.call-done.gate_ref, bf16[2560,800]{1,0:T(8,128)(2,1)} %bitcast.49, bf16[800,2560]{1,0:T(8,128)(2,1)S(1)} %copy-done.4), custom_call_target="tpu_custom_call" | custom-call | flops 6291456000 | bytes 16777216 | tf_op jit(solution)/shard_map/pallas_call | solution.py:207
  322.9 0.8 copy.49
  (82 shorter events, 1.2 us)
Async XLA Ops:
  7.2 19.8 %copy-start = (bf16[768,1920]{1,0:T(8,128)(2,1)S(1)}, bf16[768,1920]{1,0:T(8,128)(2,1)}, u32[]{:S(2)}) copy-start(bf16[768,1920]{1,0:T(8,128)(2,1)} %param.23) | copy-start | bytes 8847364
  7.2 4.3 %copy-start.21 = (s32[4]{0:T(128)S(1)}, s32[4]{0:T(128)}, u32[]{:S(2)}) copy-start(s32[4]{0:T(128)} %param.37) | copy-start | bytes 52
  7.2 6.8 %copy-start.22 = (s32[8]{0:T(128)S(1)}, s32[8]{0:T(128)}, u32[]{:S(2)}) copy-start(s32[8]{0:T(128)} %param.36) | copy-start | bytes 100
  7.2 9.6 %copy-start.18 = (bf16[2560]{0:T(1024)(128)(2,1)S(1)}, bf16[2560]{0:T(1024)(128)(2,1)}, u32[]{:S(2)}) copy-start(bf16[2560]{0:T(1024)(128)(2,1)} %param.20) | copy-start | bytes 15364
  7.2 76.0 %all-gather.4.cloned.1.call-start = ((), (), s32[]{:S(2)}) async-start(), calls=%async_computation | async-start | bytes 3538944 | tf_op jit(solution)/shard_map/all_gather | solution.py:313
  9.3 232.4 %all-gather.8.cloned.1.call-start = ((), (), s32[]{:S(2)}) async-start(), calls=%async_computation.2 | async-start | bytes 5160960 | tf_op jit(solution)/shard_map/all_gather | solution.py:362
  10.1 10.4 %copy-start.23 = (bf16[256]{0:T(256)(128)(2,1)S(1)}, bf16[256]{0:T(256)(128)(2,1)}, u32[]{:S(2)}) copy-start(bf16[256]{0:T(256)(128)(2,1)} %param.25) | copy-start | bytes 1540
  10.1 238.7 %all-gather.6.cloned.1.call-start = ((), (), s32[]{:S(2)}) async-start(), calls=%async_computation.1 | async-start | bytes 5160960 | tf_op jit(solution)/shard_map/all_gather | solution.py:360
  10.8 11.0 %copy-start.24 = (s32[4]{0:T(128)S(1)}, s32[4]{0:T(128)}, u32[]{:S(2)}) copy-start(s32[4]{0:T(128)} %param.35) | copy-start | bytes 52
  20.5 0.7 copy-start.13
  23.7 3.2 copy-start.20
  27.6 2.9 copy-start.15
  27.9 3.7 %copy-start.12 = (bf16[128,1920]{0,1:T(8,128)(2,1)}, bf16[128,1920]{0,1:T(8,128)(2,1)S(1)}, u32[]{:S(2)}) copy-start(bf16[128,1920]{0,1:T(8,128)(2,1)S(1)} %copy.39) | copy-start | bytes 1474564
  51.0 23.1 %copy-start.19 = (bf16[2560]{0:T(1024)(128)(2,1)S(1)}, bf16[2560]{0:T(1024)(128)(2,1)}, u32[]{:S(2)}) copy-start(bf16[2560]{0:T(1024)(128)(2,1)} %param.29) | copy-start | bytes 15364
  51.0 23.2 %copy-start.16 = (bf16[128,256]{0,1:T(8,128)(2,1)S(1)}, bf16[128,256]{0,1:T(8,128)(2,1)}, u32[]{:S(2)}) copy-start(bf16[128,256]{0,1:T(8,128)(2,1)} %multiply_convert_fusion.2) | copy-start | bytes 196612
  74.8 1.9 copy-start.17
  74.8 2.0 copy-start.10
  74.8 2.2 copy-start.14
  76.6 1.1 copy-start.9
  83.2 2.4 copy-start.8
  85.6 3.5 %copy-start.6 = (bf16[320,800]{1,0:T(8,128)(2,1)S(1)}, bf16[320,800]{1,0:T(8,128)(2,1)}, u32[]{:S(2)}) copy-start(bf16[320,800]{1,0:T(8,128)(2,1)} %shard_ref.1) | copy-start | bytes 1536004
  89.1 149.2 %slice-start = ((s8[6553600]{0:T(1024)(128)(4,1)}), s8[4194304]{0:T(1024)(128)(4,1)S(1)}, s32[]{:S(2)}) async-start(s8[6553600]{0:T(1024)(128)(4,1)} %bitcast.36), calls=%async_computation.3 | async-start | bytes 8388608
  89.1 148.6 %copy-start.11 = (bf16[256,1280]{0,1:T(8,128)(2,1)S(1)}, bf16[256,1280]{0,1:T(8,128)(2,1)}, u32[]{:S(2)}) copy-start(bf16[256,1280]{0,1:T(8,128)(2,1)} %copy.45) | copy-start | bytes 1966084
  89.1 149.2 %slice-start.1 = ((s8[6553600]{0:T(1024)(128)(4,1)}), s8[2359296]{0:T(1024)(128)(4,1)S(1)}, s32[]{:S(2)}) async-start(s8[6553600]{0:T(1024)(128)(4,1)} %bitcast.36), calls=%async_computation.4 | async-start | bytes 4718592
  237.7 1.1 copy-start.7
  239.8 0.8 copy-start.2
  248.8 1.1 copy-start.3
  249.9 2.2 copy-start.4
  252.1 1.1 copy-start.5
  253.2 70.6 %copy-start.1 = (bf16[768,1920]{1,0:T(8,128)(2,1)S(1)}, bf16[768,1920]{1,0:T(8,128)(2,1)}, u32[]{:S(2)}) copy-start(bf16[768,1920]{1,0:T(8,128)(2,1)} %param.23) | copy-start | bytes 8847364
Sparse Core Ops, SparseCore 0:
  9.7 43.1 all-gather.3
  54.6 74.9 all-gather.7
  131.2 100.8 all-gather.5
